TPU v7x, 32 devices: a whole 2x2x4 slice. The times are simulated.
32 devices in a mesh: req: 8 (over z, x), tile: 4 (over y, core).
Axes of the slice: x: 2, y: 2, z: 4, core: 2. Of those that a mesh axis runs over, the one named last changes fastest.
Arguments:
- latents: bfloat16 [256, 16, 128], P(('req', 'tile')), may hold values from -6 to 6
- piece_dest: int32 [256], replicated, may hold values from 0 to 255, as said below
- frames: int32 [8], replicated, may hold values from 1 to 2
- heights: int32 [8], replicated, may hold values from 8 to 16
- widths: int32 [8], replicated, may hold values from 64 to 128
- w_in: bfloat16 [3, 3, 3, 384, 16], replicated, may hold values from -0.3125 to 0.3125
- b_in: float32 [384], replicated, may hold values from -3 to 3
- gain_norm: float32 [384], replicated, may hold values from 0.5 to 1.5
- w_res: bfloat16 [3, 3, 3, 384, 384], replicated, may hold values from -0.0625 to 0.0625
- b_res: float32 [384], replicated, may hold values from -3 to 3
- w_time: bfloat16 [3, 768, 384], replicated, may hold values from -0.1875 to 0.1875
- b_time: float32 [768], replicated, may hold values from -3 to 3
- w_up: bfloat16 [3, 3, 192, 384], replicated, may hold values from -0.109375 to 0.109375
- b_up: float32 [192], replicated, may hold values from -3 to 3
Outputs:
- decoded: bfloat16 [8, 192, 4, 32, 256], P('req', None, None, 'tile')
Inputs may be any that keep to these rules, and one draw needn't show every extreme that they name: piece_dest is a permutation of the decoder slots. Requests are packed one after another in a drawn order, each request's rows frame after frame and row after row, so the 8 rows of one device are consecutive rows of one request and no device sends more than 4 rows to one device.
All inputs are finite; a program needn't handle non-finite values.
Results may differ from a plain program's by a relative error of at most 0.0075.
Values may be sent and summed in bfloat16 or wider, within the bound.
A program may use at most 192 MiB of HBM per device.

v0:
```python
import jax
import jax.numpy as jnp
from jax import lax
from jax.sharding import PartitionSpec as P

LFRAMES = 2


def with_halo(cells, sides, width):
    for axis, dim in sides:
        count = lax.axis_size(axis)
        ends = count - 1
        head = lax.slice_in_dim(cells, 0, width, axis=dim)
        tail = lax.slice_in_dim(cells, cells.shape[dim] - width, cells.shape[dim], axis=dim)
        cells = jnp.concatenate(
            [
                lax.ppermute(tail, axis, [(i, (i + 1) % count) for i in range(ends)]),
                cells,
                lax.ppermute(head, axis, [((i + 1) % count, i) for i in range(ends)]),
            ],
            axis=dim,
        )
    return cells


def causal_conv(extended, weight, offsets):
    frame_count = extended.shape[1]
    row_count = extended.shape[2] - 2
    col_count = extended.shape[3]
    padded = jnp.pad(extended, ((0, 0), (2, 0), (0, 0), (1, 1)))
    shifted = jnp.stack([padded[..., tap_c : tap_c + col_count] for tap_c in range(3)], axis=0)
    summed = jnp.zeros((weight.shape[3], frame_count, row_count, col_count), jnp.float32)
    for tap_t in range(3):
        for tap_r in range(3):
            kernel = jnp.transpose(weight[tap_t, tap_r], (1, 0, 2))
            summed = summed + jnp.einsum(
                "okc,kcthw->othw",
                kernel,
                shifted[:, :, tap_t : tap_t + frame_count, tap_r : tap_r + row_count, :],
                preferred_element_type=jnp.float32,
            )
    return summed + offsets[:, None, None, None]


def time_double(features, cell_mask, w_time, b_time):
    channels, frame_count = (features.shape[0], features.shape[1])
    padded = jnp.pad(features, ((0, 0), (2, 0), (0, 0), (0, 0)))
    twice = jnp.zeros((2 * channels,) + features.shape[1:], jnp.float32)
    for tap_t in range(3):
        twice = twice + jnp.einsum(
            "oc,cthw->othw",
            w_time[tap_t],
            padded[:, tap_t : tap_t + frame_count],
            preferred_element_type=jnp.float32,
        )
    twice = twice + b_time[:, None, None, None]
    doubled = jnp.stack([twice[:channels], twice[channels:]], axis=2)
    doubled = doubled.reshape((channels, 2 * frame_count) + features.shape[2:])
    return (doubled * jnp.repeat(cell_mask, 2, axis=0)).astype(jnp.bfloat16)


def on_device(
    latents,
    piece_dest,
    frames,
    heights,
    widths,
    w_in,
    b_in,
    gain_norm,
    w_res,
    b_res,
    w_time,
    b_time,
    w_up,
    b_up,
):
    tile_count = lax.axis_size("tile")
    group_id = lax.axis_index("req")
    tile_id = lax.axis_index("tile")
    device_id = group_id * tile_count + tile_id
    slot_count, channels, col_count = latents.shape
    rows_dev = slot_count // LFRAMES
    flattened = latents.reshape(slot_count, channels * col_count)
    wanted = device_id * slot_count + jnp.arange(slot_count, dtype=jnp.int32)
    selector = (piece_dest[None, :] == wanted[:, None]).astype(jnp.bfloat16)
    latent_grid = jnp.dot(
        selector,
        lax.all_gather(flattened, ("req", "tile"), axis=0, tiled=True),
        preferred_element_type=jnp.float32,
    )
    latent_grid = latent_grid.reshape(LFRAMES, rows_dev, channels, col_count).transpose(2, 0, 1, 3)
    frame_ids = jnp.arange(LFRAMES, dtype=jnp.int32)
    row_ids = tile_id * rows_dev - 1 + jnp.arange(rows_dev + 2, dtype=jnp.int32)
    col_ids = jnp.arange(col_count, dtype=jnp.int32)
    mask_extended = (
        (frame_ids < frames[group_id])[:, None, None]
        & ((row_ids >= 0) & (row_ids < heights[group_id]))[None, :, None]
        & (col_ids < widths[group_id])[None, None, :]
    ).astype(jnp.float32)
    mask_core = mask_extended[:, 1:-1, :]
    masked_input = (latent_grid * mask_core).astype(jnp.bfloat16)
    input_rim = with_halo(masked_input, (("tile", 2),), 1)
    first = causal_conv(input_rim, w_in, b_in).astype(jnp.bfloat16)
    first_f = first.astype(jnp.float32)
    scaled = (
        first_f
        * lax.rsqrt(jnp.mean(first_f * first_f, axis=0, keepdims=True) + 1e-06)
        * gain_norm[:, None, None, None]
    )
    normed = (jax.nn.silu(scaled) * mask_core).astype(jnp.bfloat16)
    normed_rim = with_halo(normed, (("tile", 2),), 1)
    block = (first_f + causal_conv(normed_rim, w_res, b_res)).astype(jnp.bfloat16)
    timed = time_double(block, mask_core, w_time, b_time)
    timed_rim = with_halo(timed, (("tile", 2),), 1)
    out_rows = 2 * rows_dev
    out_cols = 2 * col_count
    taller = jnp.repeat(timed_rim, 2, axis=2)[:, :, 1:-1, :]
    widened = jnp.repeat(taller, 2, axis=3)
    padded = jnp.pad(widened, ((0, 0), (0, 0), (0, 0), (1, 1)))
    shifted = jnp.stack([padded[..., tap_c : tap_c + out_cols] for tap_c in range(3)], axis=0)
    summed = jnp.zeros((w_up.shape[2], timed_rim.shape[1], out_rows, out_cols), jnp.float32)
    for tap_r in range(3):
        kernel = jnp.transpose(w_up[tap_r], (1, 0, 2))
        summed = summed + jnp.einsum(
            "okc,kcthw->othw",
            kernel,
            shifted[:, :, :, tap_r : tap_r + out_rows, :],
            preferred_element_type=jnp.float32,
        )
    summed = summed + b_up[:, None, None, None]
    out_mask = jnp.repeat(jnp.repeat(jnp.repeat(mask_core, 2, axis=0), 2, axis=1), 2, axis=2)
    decoded = (summed * out_mask).astype(jnp.bfloat16)
    return decoded[None]


def solution(mesh):
    return jax.shard_map(
        on_device,
        mesh=mesh,
        in_specs=(
            P(("req", "tile"), None, None),
            P(),
            P(),
            P(),
            P(),
            P(),
            P(),
            P(),
            P(),
            P(),
            P(),
            P(),
            P(),
            P(),
        ),
        out_specs=P("req", None, None, "tile", None),
        check_vma=False,
    )
```

profile of v0, /device:TPU:1, one launch (start us, length us, event | category | flops | bytes accessed | tf_op | source)
XLA Modules:
  0.0 268.3 jit_solution(6755693431236418709)
XLA Ops:
  13.9 52.7 %all-gather.2.cloned.1.call-done = bf16[256,2048]{1,0:T(8,128)(2,1)} async-done(((bf16[8,2048]{1,0:T(8,128)(2,1)}), bf16[256,2048]{1,0:T(8,128)(2,1)}) %all-gather.2.cloned.1.call-update) | async-done | bytes 1048592 | tf_op jit(solution)/shard_map/all_gather | solution.py:89
  68.2 3.2 %collective-permute-start = (bf16[16,2,1,128]{3,0,2,1:T(8,128)(2,1)S(1)}, bf16[16,2,1,128]{3,0,2,1:T(8,128)(2,1)S(1)}, u32[]{:S(2)}, u32[]{:S(2)}) collective-permute-start(bf16[16,2,1,128]{3,0,2,1:T(8,128)(2,1)S(1)} %get-tuple-element.28), channel_id=1, source_target_pairs={{0,1},{1,2},{2,3},{4,5},{5,6},{6,7},{8,9},{9,10},{10,11},{12,13},{... | collective-permute-start | bytes 24584 | tf_op jit(solution)/shard_map/ppermute | solution.py:17
  73.3 3.0 %collective-permute-done.1 = bf16[16,2,1,128]{3,0,2,1:T(8,128)(2,1)S(1)} collective-permute-done((bf16[16,2,1,128]{3,0,2,1:T(8,128)(2,1)S(1)}, bf16[16,2,1,128]{3,0,2,1:T(8,128)(2,1)S(1)}, u32[]{:S(2)}, u32[]{:S(2)}) %collective-permute-start.1) | collective-permute-done | bytes 8224 | tf_op jit(solution)/shard_map/ppermute | solution.py:19
  95.4 8.4 %fusion.160 = (bf16[3,384,2,4,128]{1,4,3,2,0:T(8,128)(2,1)}, bf16[3,384,2,4,128]{1,4,3,2,0:T(8,128)(2,1)}, bf16[3,384,2,4,128]{1,4,3,2,0:T(8,128)(2,1)}, bf16[3,...) fusion(bf16[3,384,4,6,128]{1,4,3,2,0:T(8,128)(2,1)S(1)} %pad_ma, ...), kind=kLoop, calls=%fused_computation.194 | loop fusion | bytes 42467328 | tf_op jit(solution)/shard_map/slice | solution.py:39
  103.8 3.5 %fusion.57 = f32[2,4,128,384]{3,2,0,1:T(8,128)S(1)} fusion(bf16[3,384,2,4,128]{1,4,3,2,0:T(8,128)(2,1)} %get-tuple-element.7, bf16[3,3,3,384,384]{4,3,2,1,0:T(8,128)(2,1)} %param.22), kind=kOutput, calls=%fused_computation.92 | convolution fusion | flops 905969664 | bytes 4816896 | tf_op jit(solution)/shard_map/okc,kcthw->othw/dot_general | solution.py:36
  107.3 2.8 %fusion.60 = f32[2,4,128,384]{3,2,0,1:T(8,128)S(1)} fusion(bf16[3,384,2,4,128]{1,4,3,2,0:T(8,128)(2,1)S(1)} %copy-done.9, bf16[3,3,3,384,384]{4,3,2,1,0:T(8,128)(2,1)} %param.22), kind=kOutput, calls=%fused_computation.93 | convolution fusion | flops 905969664 | bytes 4816896 | tf_op jit(solution)/shard_map/okc,kcthw->othw/dot_general | solution.py:36
  110.1 2.8 %fusion.63 = f32[2,4,128,384]{3,2,0,1:T(8,128)S(1)} fusion(bf16[3,384,2,4,128]{1,4,3,2,0:T(8,128)(2,1)S(1)} %copy-done.8, bf16[3,3,3,384,384]{4,3,2,1,0:T(8,128)(2,1)} %param.22), kind=kOutput, calls=%fused_computation.94 | convolution fusion | flops 905969664 | bytes 4816896 | tf_op jit(solution)/shard_map/okc,kcthw->othw/dot_general | solution.py:36
  112.9 2.8 %fusion.66 = f32[2,4,128,384]{3,2,0,1:T(8,128)S(1)} fusion(bf16[3,384,2,4,128]{1,4,3,2,0:T(8,128)(2,1)S(1)} %copy-done.7, bf16[3,3,3,384,384]{4,3,2,1,0:T(8,128)(2,1)} %param.22), kind=kOutput, calls=%fused_computation.95 | convolution fusion | flops 905969664 | bytes 4816896 | tf_op jit(solution)/shard_map/okc,kcthw->othw/dot_general | solution.py:36
  115.7 2.8 %fusion.69 = f32[2,4,128,384]{3,2,0,1:T(8,128)S(1)} fusion(bf16[3,384,2,4,128]{1,4,3,2,0:T(8,128)(2,1)S(1)} %copy-done.6, bf16[3,3,3,384,384]{4,3,2,1,0:T(8,128)(2,1)} %param.22), kind=kOutput, calls=%fused_computation.96 | convolution fusion | flops 905969664 | bytes 4816896 | tf_op jit(solution)/shard_map/okc,kcthw->othw/dot_general | solution.py:36
  118.5 2.8 %fusion.72 = f32[2,4,128,384]{3,2,0,1:T(8,128)S(1)} fusion(bf16[3,384,2,4,128]{1,4,3,2,0:T(8,128)(2,1)S(1)} %copy-done.5, bf16[3,3,3,384,384]{4,3,2,1,0:T(8,128)(2,1)} %param.22), kind=kOutput, calls=%fused_computation.97 | convolution fusion | flops 905969664 | bytes 4816896 | tf_op jit(solution)/shard_map/okc,kcthw->othw/dot_general | solution.py:36
  121.3 2.8 %fusion.75 = f32[2,4,128,384]{3,2,0,1:T(8,128)S(1)} fusion(bf16[3,384,2,4,128]{1,4,3,2,0:T(8,128)(2,1)S(1)} %copy-done.4, bf16[3,3,3,384,384]{4,3,2,1,0:T(8,128)(2,1)} %param.22), kind=kOutput, calls=%fused_computation.98 | convolution fusion | flops 905969664 | bytes 4816896 | tf_op jit(solution)/shard_map/okc,kcthw->othw/dot_general | solution.py:36
  124.1 2.8 %fusion.78 = f32[2,4,128,384]{3,2,0,1:T(8,128)S(1)} fusion(bf16[3,384,2,4,128]{1,4,3,2,0:T(8,128)(2,1)S(1)} %copy-done.3, bf16[3,3,3,384,384]{4,3,2,1,0:T(8,128)(2,1)} %param.22), kind=kOutput, calls=%fused_computation.99 | convolution fusion | flops 905969664 | bytes 4816896 | tf_op jit(solution)/shard_map/okc,kcthw->othw/dot_general | solution.py:36
  126.9 2.6 fusion.81
  147.2 4.1 %collective-permute-done.5 = bf16[384,4,1,128]{3,0,2,1:T(8,128)(2,1)S(1)} collective-permute-done((bf16[384,4,1,128]{3,0,2,1:T(8,128)(2,1)S(1)}, bf16[384,4,1,128]{3,0,2,1:T(8,128)(2,1)S(1)}, u32[]{:S(2)}, u32[]{:S(2)}) %collective-permute-start.5) | collective-permute-done | bytes 393248 | tf_op jit(solution)/shard_map/ppermute | solution.py:19
  152.9 4.1 %copy.68 = bf16[384,4,6,128]{0,1,3,2:T(4,128)(2,1)S(1)} copy(bf16[384,4,6,128]{3,0,2,1:T(8,128)(2,1)} %pad_maximum_fusion.3) | data formatting | bytes 4718592 | tf_op jit(solution)/shard_map/concatenate | solution.py:15
  160.4 4.1 %broadcast_in_dim.14 = bf16[384,4,10,128,2]{0,1,4,3,2:T(4,128)(2,1)} broadcast(bf16[384,4,10,128]{0,1,3,2:T(4,128)(2,1)S(1)} %slice.290), dimensions={0,1,2,3} | broadcast | bytes 11796480 | tf_op jit(solution)/shard_map/broadcast_in_dim | solution.py:119
  164.5 13.0 %copy.69 = bf16[384,4,10,256]{3,0,2,1:T(8,128)(2,1)} copy(bf16[384,4,10,256]{0,1,3,2:T(4,128)(2,1)} %bitcast.377) | data formatting | bytes 15728640 | tf_op jit(solution)/shard_map/reshape | solution.py:119
  177.5 14.4 %fusion.6 = (bf16[1,384,4,10,256]{4,1,0,3,2:T(8,128)(2,1)}, bf16[1,384,4,10,256]{4,1,0,3,2:T(8,128)(2,1)}) fusion(bf16[384,4,10,256]{3,0,2,1:T(8,128)(2,1)} %copy.69), kind=kLoop, calls=%fused_computation.9 | loop fusion | bytes 23592960 | tf_op jit(solution)/shard_map/stack | solution.py:121
  191.9 13.0 %copy.71 = bf16[1,384,4,10,256]{4,1,0,3,2:T(8,128)(2,1)} copy(bf16[1,384,4,10,256]{1,2,4,3,0:T(4,128)(2,1)} %bitcast.378) | data formatting | bytes 15728640 | tf_op jit(solution)/shard_map/stack | solution.py:121
  205.0 19.8 %pad_maximum_fusion = bf16[3,384,4,10,256]{4,1,0,3,2:T(8,128)(2,1)} fusion(bf16[1,384,4,10,256]{4,1,0,3,2:T(8,128)(2,1)} %get-tuple-element.6, bf16[1,384,4,10,256]{4,1,0,3,2:T(8,128)(2,1)} %copy.71, bf16[1,384,4,10,256]{4,1,0,3,2:T(8,128)(2,1)} %get-tuple-element.5), kind=kLoop, calls=%fused_computation | loop fusion | flops 23592960 | bytes 47185920 | tf_op jit(solution)/shard_map/stack | solution.py:121
  224.8 10.3 %fusion = f32[4,8,256,192,1]{2,3,4,1,0:T(8,128)} fusion(bf16[3,384,4,10,256]{4,1,0,3,2:T(8,128)(2,1)} %pad_maximum_fusion, bf16[3,3,192,384]{3,2,1,0:T(8,128)(2,1)S(1)} %copy-done.17), kind=kOutput, calls=%fused_computation.1 | convolution fusion | flops 3623878656 | bytes 25608192 | tf_op jit(solution)/shard_map/okc,kcthw->othw/dot_general | solution.py:125
  235.1 10.4 %fusion.2 = f32[4,8,256,192,1]{2,3,4,1,0:T(8,128)} fusion(bf16[3,384,4,10,256]{4,1,0,3,2:T(8,128)(2,1)} %pad_maximum_fusion, bf16[3,3,192,384]{3,2,1,0:T(8,128)(2,1)S(1)} %copy-done.17), kind=kOutput, calls=%fused_computation.3 | convolution fusion | flops 3623878656 | bytes 25608192 | tf_op jit(solution)/shard_map/okc,kcthw->othw/dot_general | solution.py:125
  245.5 12.4 %fusion.16 = bf16[1,192,4,8,256]{4,1,3,2,0:T(8,128)(2,1)S(1)} fusion(f32[4,8,256,192,1]{2,3,4,1,0:T(8,128)} %fusion, f32[4,8,256,192,1]{2,3,4,1,0:T(8,128)} %fusion.2, f32[4,8,256]{2,1,0:T(8,128)S(1)} %copy-done.12, f32[192]{0:T(256)S(1)} %copy-done.18, bf16[3,384,4,10,256]{4,1,0,3,2:T(8,128)(2,1)} %pad_maximum_fusion, ...), kind=kOutput, calls=%fused_computation.25 | convolution fusion | flops 3631742976 | bytes 35079168 | tf_op jit(solution)/shard_map/okc,kcthw->othw/dot_general | solution.py:125
  257.9 3.5 %copy.74 = bf16[1,192,4,8,256]{4,3,2,1,0:T(8,128)(2,1)} copy(bf16[1,192,4,8,256]{4,1,3,2,0:T(8,128)(2,1)S(1)} %fusion.16) | data formatting | bytes 6291456 | tf_op jit(solution)/shard_map/broadcast_in_dim | solution.py:134
  (98 shorter events, 52.3 us)
Async XLA Ops:
  6.5 70.1 %copy-start.11 = (bf16[3,3,3,384,16]{3,4,2,1,0:T(8,128)(2,1)S(1)}, bf16[3,3,3,384,16]{3,4,2,1,0:T(8,128)(2,1)}, u32[]{:S(2)}) copy-start(bf16[3,3,3,384,16]{3,4,2,1,0:T(8,128)(2,1)} %param.19) | copy-start | bytes 995332
  6.5 60.0 %all-gather.2.cloned.1.call-start = ((), (), s32[]{:S(2)}) async-start(), calls=%async_computation | async-start | bytes 1081344 | tf_op jit(solution)/shard_map/all_gather | solution.py:89
  68.2 5.2 %collective-permute-start = (bf16[16,2,1,128]{3,0,2,1:T(8,128)(2,1)S(1)}, bf16[16,2,1,128]{3,0,2,1:T(8,128)(2,1)S(1)}, u32[]{:S(2)}, u32[]{:S(2)}) collective-permute-start(bf16[16,2,1,128]{3,0,2,1:T(8,128)(2,1)S(1)} %get-tuple-element.28), channel_id=1, source_target_pairs={{0,1},{1,2},{2,3},{4,5},{5,6},{6,7},{8,9},{9,10},{10,11},{12,13},{... | collective-permute-start | bytes 24584 | tf_op jit(solution)/shard_map/ppermute | solution.py:17
  71.4 5.0 %collective-permute-start.1 = (bf16[16,2,1,128]{3,0,2,1:T(8,128)(2,1)S(1)}, bf16[16,2,1,128]{3,0,2,1:T(8,128)(2,1)S(1)}, u32[]{:S(2)}, u32[]{:S(2)}) collective-permute-start(bf16[16,2,1,128]{3,0,2,1:T(8,128)(2,1)S(1)} %get-tuple-element.29), channel_id=1, source_target_pairs={{1,0},{2,1},{3,2},{5,4},{6,5},{7,6},{9,8},{10,9},{11,10},{13,12},{... | collective-permute-start | bytes 24584 | tf_op jit(solution)/shard_map/ppermute | solution.py:19
  79.8 1.1 copy-start.15
  81.5 6.4 %collective-permute-start.2 = (bf16[384,2,1,128]{0,3,2,1:T(8,128)(2,1)S(1)}, bf16[384,2,1,128]{0,3,2,1:T(8,128)(2,1)S(1)}, u32[]{:S(2)}, u32[]{:S(2)}) collective-permute-start(bf16[384,2,1,128]{0,3,2,1:T(8,128)(2,1)S(1)} %get-tuple-element.23), channel_id=1, source_target_pairs={{0,1},{1,2},{2,3},{4,5},{5,6},{6,7},{8,9},{9,10},{10,11},{12,13},{... | collective-permute-start | bytes 589832 | tf_op jit(solution)/shard_map/ppermute | solution.py:17
  83.5 7.0 %collective-permute-start.3 = (bf16[384,2,1,128]{0,3,2,1:T(8,128)(2,1)S(1)}, bf16[384,2,1,128]{0,3,2,1:T(8,128)(2,1)S(1)}, u32[]{:S(2)}, u32[]{:S(2)}) collective-permute-start(bf16[384,2,1,128]{0,3,2,1:T(8,128)(2,1)S(1)} %get-tuple-element.24), channel_id=1, source_target_pairs={{1,0},{2,1},{3,2},{5,4},{6,5},{7,6},{9,8},{10,9},{11,10},{13,12},{... | collective-permute-start | bytes 589832 | tf_op jit(solution)/shard_map/ppermute | solution.py:19
  103.8 3.5 %copy-start.9 = (bf16[3,384,2,4,128]{1,4,3,2,0:T(8,128)(2,1)S(1)}, bf16[3,384,2,4,128]{1,4,3,2,0:T(8,128)(2,1)}, u32[]{:S(2)}) copy-start(bf16[3,384,2,4,128]{1,4,3,2,0:T(8,128)(2,1)} %get-tuple-element.15) | copy-start | bytes 7077892
  107.3 2.8 %copy-start.8 = (bf16[3,384,2,4,128]{1,4,3,2,0:T(8,128)(2,1)S(1)}, bf16[3,384,2,4,128]{1,4,3,2,0:T(8,128)(2,1)}, u32[]{:S(2)}) copy-start(bf16[3,384,2,4,128]{1,4,3,2,0:T(8,128)(2,1)} %get-tuple-element.14) | copy-start | bytes 7077892
  110.1 2.8 %copy-start.7 = (bf16[3,384,2,4,128]{1,4,3,2,0:T(8,128)(2,1)S(1)}, bf16[3,384,2,4,128]{1,4,3,2,0:T(8,128)(2,1)}, u32[]{:S(2)}) copy-start(bf16[3,384,2,4,128]{1,4,3,2,0:T(8,128)(2,1)} %get-tuple-element.13) | copy-start | bytes 7077892
  112.9 2.8 %copy-start.6 = (bf16[3,384,2,4,128]{1,4,3,2,0:T(8,128)(2,1)S(1)}, bf16[3,384,2,4,128]{1,4,3,2,0:T(8,128)(2,1)}, u32[]{:S(2)}) copy-start(bf16[3,384,2,4,128]{1,4,3,2,0:T(8,128)(2,1)} %get-tuple-element.12) | copy-start | bytes 7077892
  115.7 2.8 %copy-start.5 = (bf16[3,384,2,4,128]{1,4,3,2,0:T(8,128)(2,1)S(1)}, bf16[3,384,2,4,128]{1,4,3,2,0:T(8,128)(2,1)}, u32[]{:S(2)}) copy-start(bf16[3,384,2,4,128]{1,4,3,2,0:T(8,128)(2,1)} %get-tuple-element.11) | copy-start | bytes 7077892
  118.5 2.8 %copy-start.4 = (bf16[3,384,2,4,128]{1,4,3,2,0:T(8,128)(2,1)S(1)}, bf16[3,384,2,4,128]{1,4,3,2,0:T(8,128)(2,1)}, u32[]{:S(2)}) copy-start(bf16[3,384,2,4,128]{1,4,3,2,0:T(8,128)(2,1)} %get-tuple-element.10) | copy-start | bytes 7077892
  121.3 2.8 %copy-start.3 = (bf16[3,384,2,4,128]{1,4,3,2,0:T(8,128)(2,1)S(1)}, bf16[3,384,2,4,128]{1,4,3,2,0:T(8,128)(2,1)}, u32[]{:S(2)}) copy-start(bf16[3,384,2,4,128]{1,4,3,2,0:T(8,128)(2,1)} %get-tuple-element.9) | copy-start | bytes 7077892
  124.1 2.8 %copy-start.2 = (bf16[3,384,2,4,128]{1,4,3,2,0:T(8,128)(2,1)S(1)}, bf16[3,384,2,4,128]{1,4,3,2,0:T(8,128)(2,1)}, u32[]{:S(2)}) copy-start(bf16[3,384,2,4,128]{1,4,3,2,0:T(8,128)(2,1)} %get-tuple-element.8) | copy-start | bytes 7077892
  126.9 2.7 copy-start.16
  129.6 1.5 copy-start.10
  138.2 1.1 copy-start
  140.1 11.1 %copy-start.1 = (bf16[384,4,4,128]{3,0,2,1:T(8,128)(2,1)S(1)}, bf16[384,4,4,128]{3,0,2,1:T(8,128)(2,1)}, u32[]{:S(2)}) copy-start(bf16[384,4,4,128]{3,0,2,1:T(8,128)(2,1)} %copy-done) | copy-start | bytes 4718596
  140.1 7.1 %collective-permute-start.4 = (bf16[384,4,1,128]{3,0,2,1:T(8,128)(2,1)}, bf16[384,4,1,128]{3,0,2,1:T(8,128)(2,1)S(1)}, u32[]{:S(2)}, u32[]{:S(2)}) collective-permute-start(bf16[384,4,1,128]{3,0,2,1:T(8,128)(2,1)} %get-tuple-element.21), channel_id=1, source_target_pairs={{0,1},{1,2},{2,3},{4,5},{5,6},{6,7},{8,9},{9,10},{10,11},{12,13},{... | collective-permute-start | bytes 1179656 | tf_op jit(solution)/shard_map/ppermute | solution.py:17
  142.1 9.1 %collective-permute-start.5 = (bf16[384,4,1,128]{3,0,2,1:T(8,128)(2,1)S(1)}, bf16[384,4,1,128]{3,0,2,1:T(8,128)(2,1)S(1)}, u32[]{:S(2)}, u32[]{:S(2)}) collective-permute-start(bf16[384,4,1,128]{3,0,2,1:T(8,128)(2,1)S(1)} %get-tuple-element.22), channel_id=1, source_target_pairs={{1,0},{2,1},{3,2},{5,4},{6,5},{7,6},{9,8},{10,9},{11,10},{13,12},{... | collective-permute-start | bytes 1179656 | tf_op jit(solution)/shard_map/ppermute | solution.py:19
  205.0 19.8 %copy-start.17 = (bf16[3,3,192,384]{3,2,1,0:T(8,128)(2,1)S(1)}, bf16[3,3,192,384]{3,2,1,0:T(8,128)(2,1)}, u32[]{:S(2)}) copy-start(bf16[3,3,192,384]{3,2,1,0:T(8,128)(2,1)} %param.26) | copy-start | bytes 3981316
  235.1 10.4 %copy-start.12 = (f32[4,8,256]{2,1,0:T(8,128)S(1)}, f32[4,8,256]{2,1,0:T(8,128)}, u32[]{:S(2)}) copy-start(f32[4,8,256]{2,1,0:T(8,128)} %copy.73) | copy-start | bytes 98308
  235.1 10.4 %copy-start.18 = (f32[192]{0:T(256)S(1)}, f32[192]{0:T(256)}, u32[]{:S(2)}) copy-start(f32[192]{0:T(256)} %param.27) | copy-start | bytes 2308
  (2 other events, 1.8 us)
Sparse Core Ops, SparseCore 0:
  10.2 56.3 all-gather.1
where the time goes:
time: 270 us; the launch traced here: 268 us
  local copies, waits for them, and re-layouts  77 us (29%)
  matrix products  68.5 us (25%)
  waiting for transfers between devices  63.8 us (24%)
  other arithmetic  31 us (11%)
  between operations  14 us (5%)
  starting transfers between devices  13.9 us (5%)
    all_gather x1, waiting for transfers between devices, on_device(): lax.all_gather(flattened, ('req', 'tile'), axis=0, tiled=True)  52.7 us
    dot_general x3, matrix products, on_device(): jnp.einsum('okc,kcthw->othw', kernel, shifted[:, :, :, tap_r:tap_r + out_...  33.1 us
    dot_general x18, matrix products, causal_conv(): jnp.einsum('okc,kcthw->othw', kernel, shifted[:, :, tap_t:tap_t + frame_c...  29.7 us
    another operation x2, local copies, waits for them, and re-layouts, on_device(): jnp.stack([padded[..., tap_c:tap_c + out_cols] for tap_c in range(3)], ax...  27.4 us
    another operation x1, other arithmetic, on_device(): jnp.stack([padded[..., tap_c:tap_c + out_cols] for tap_c in range(3)], ax...  19.8 us
    reshape x1, local copies, waits for them, and re-layouts, on_device(): widened = jnp.repeat(taller, 2, axis=3)  13 us
    ppermute x3, waiting for transfers between devices, with_halo(): lax.ppermute(head, axis, [((i + 1) % count, i) for i in range(ends)])  9.62 us
    slice x1, local copies, waits for them, and re-layouts, causal_conv(): shifted[:, :, tap_t:tap_t + frame_count, tap_r:tap_r + row_count, :]  8.36 us
  transfers between devices with their start and end apart: 7, of which 5 were waited for; matrix products, arithmetic and copies ran while one was open for 3% of the time, Pallas kernels for 0%

commit v1 on v0

v1 whole, which is shorter than its diff:
```python
import functools

import jax
import jax.numpy as jnp
from jax import lax
from jax.experimental import pallas as pl
from jax.experimental.pallas import tpu as pltpu
from jax.sharding import PartitionSpec as P

LFRAMES = 2
MESH = pl.DeviceIdType.MESH
F32 = jnp.float32
BF16 = jnp.bfloat16


def route_kernel(
    n_req, n_tile, dest_ref, lat_ref, out_ref, buf, sel, send_sem, recv_sem, side_send, side_recv
):
    g = lax.axis_index("req")
    t = lax.axis_index("tile")
    half = n_tile // 2
    slots = lat_ref.shape[0]
    rows = slots // LFRAMES

    barrier = pltpu.get_barrier_semaphore()

    def greet(k, carry):
        other = lax.rem(g + k, n_req)
        for f in range(LFRAMES):
            source = f * half + t // 2

            @pl.when((k > 0) | (source != t))
            def _():
                pl.semaphore_signal(
                    barrier, inc=1, device_id=(other, source), device_id_type=MESH
                )

        return carry

    lax.fori_loop(0, n_req, greet, 0)

    @pl.when(t > 0)
    def _():
        pl.semaphore_signal(barrier, inc=1, device_id=(g, t - 1), device_id_type=MESH)

    @pl.when(t < n_tile - 1)
    def _():
        pl.semaphore_signal(barrier, inc=1, device_id=(g, t + 1), device_id_type=MESH)

    inner = (t + n_tile - 1) // n_tile - (t + 1) // n_tile
    pl.semaphore_wait(barrier, 2 * n_req + 2 * inner)

    frame = t // half
    first_tile = 2 * lax.rem(t, half)

    def remote(k, h):
        return pltpu.make_async_remote_copy(
            src_ref=lat_ref.at[pl.ds(h * rows, rows)],
            dst_ref=buf.at[g, frame],
            send_sem=send_sem.at[k, h],
            recv_sem=recv_sem.at[g, frame],
            device_id=(lax.rem(g + k, n_req), first_tile + h),
            device_id_type=MESH,
        )

    def local(h):
        return pltpu.make_async_copy(
            lat_ref.at[pl.ds(h * rows, rows)], buf.at[g, frame], recv_sem.at[g, frame]
        )

    def send(k, carry):
        for h in range(2):

            @pl.when((k > 0) | (first_tile + h != t))
            def _():
                remote(k, h).start()

            @pl.when((k == 0) & (first_tile + h == t))
            def _():
                local(h).start()

        return carry

    lax.fori_loop(0, n_req, send, 0)

    def arrive(s, carry):
        for f in range(LFRAMES):
            pltpu.make_async_copy(buf.at[s, f], buf.at[s, f], recv_sem.at[s, f]).wait()
        return carry

    lax.fori_loop(0, n_req, arrive, 0)

    per = slots * n_tile
    source = jnp.int32(0)
    for j in range(n_req):
        source = jnp.where(dest_ref[j * per] // per == g, j, source)
    sel[:, 3 : 3 + rows] = buf[source]

    up = pltpu.make_async_remote_copy(
        src_ref=sel.at[:, pl.ds(3, 3)],
        dst_ref=sel.at[:, pl.ds(3 + rows, 3)],
        send_sem=side_send.at[0],
        recv_sem=side_recv.at[0],
        device_id=(g, t - 1),
        device_id_type=MESH,
    )
    down = pltpu.make_async_remote_copy(
        src_ref=sel.at[:, pl.ds(rows, 3)],
        dst_ref=sel.at[:, pl.ds(0, 3)],
        send_sem=side_send.at[1],
        recv_sem=side_recv.at[1],
        device_id=(g, t + 1),
        device_id_type=MESH,
    )
    zeros = jnp.zeros((LFRAMES, 3) + lat_ref.shape[1:], BF16)

    @pl.when(t > 0)
    def _():
        up.start()

    @pl.when(t < n_tile - 1)
    def _():
        down.start()

    @pl.when(t == 0)
    def _():
        sel[:, 0:3] = zeros

    @pl.when(t == n_tile - 1)
    def _():
        sel[:, 3 + rows :] = zeros

    def sent(k, carry):
        for h in range(2):

            @pl.when((k > 0) | (first_tile + h != t))
            def _():
                remote(k, h).wait_send()

        return carry

    lax.fori_loop(0, n_req, sent, 0)

    @pl.when(t > 0)
    def _():
        up.wait_send()
        down.wait_recv()

    @pl.when(t < n_tile - 1)
    def _():
        down.wait_send()
        up.wait_recv()

    out_ref[...] = sel[...]


def route(n_req, n_tile, piece_dest, latents):
    slots, channels, cols = latents.shape
    rows = slots // LFRAMES
    return pl.pallas_call(
        functools.partial(route_kernel, n_req, n_tile),
        out_shape=jax.ShapeDtypeStruct((LFRAMES, rows + 6, channels, cols), BF16),
        in_specs=[
            pl.BlockSpec(memory_space=pltpu.SMEM),
            pl.BlockSpec(memory_space=pltpu.VMEM),
        ],
        out_specs=pl.BlockSpec(memory_space=pltpu.VMEM),
        scratch_shapes=[
            pltpu.VMEM((n_req, LFRAMES, rows, channels, cols), BF16),
            pltpu.VMEM((LFRAMES, rows + 6, channels, cols), BF16),
            pltpu.SemaphoreType.DMA((n_req, 2)),
            pltpu.SemaphoreType.DMA((n_req, LFRAMES)),
            pltpu.SemaphoreType.DMA((2,)),
            pltpu.SemaphoreType.DMA((2,)),
        ],
        compiler_params=pltpu.CompilerParams(
            collective_id=0, has_side_effects=True, vmem_limit_bytes=16 * 2**20
        ),
        name="route",
    )(piece_dest, latents)


def shift(x, by):
    width = x.shape[1]
    lane = lax.broadcasted_iota(jnp.int32, x.shape, 1)
    if by == 1:
        return jnp.where(lane == 0, 0.0, pltpu.roll(x, 1, axis=1))
    return jnp.where(lane == width - 1, 0.0, pltpu.roll(x, width - 1, axis=1))


def column(ref):
    n = ref.shape[1]
    return jnp.transpose(jnp.broadcast_to(ref[...], (128, n)))


def decode_kernel(
    frames_ref,
    heights_ref,
    widths_ref,
    grid_ref,
    w_in_ref,
    b_in_ref,
    gain_ref,
    b_res_ref,
    b_time_ref,
    b_up_ref,
    w_res_hbm,
    w_time_hbm,
    w_up_hbm,
    out_ref,
    w_in,
    wr,
    wt,
    wu_raw,
    wu,
    x_in,
    first,
    spread,
    timed,
    inter,
    perm,
    c_in,
    c_gain,
    c_res,
    c_time,
    c_up,
    sem_r,
    sem_t,
    sem_u,
):
    g = lax.axis_index("req")
    t = lax.axis_index("tile")
    channels, cols = grid_ref.shape[2], grid_ref.shape[3]
    rows = grid_ref.shape[1] - 6
    mid = w_in_ref.shape[1]
    outc = b_up_ref.shape[1]
    one = 9 * channels
    mrows = rows + 4

    copies_r = []
    for d in range(3):
        for a in range(2):
            for e in range(3):
                at = (a * 3 + e) * mid
                copies_r.append(
                    pltpu.make_async_copy(
                        w_res_hbm.at[a + 1, d, e],
                        wr.at[d, :, pl.ds(at, mid)],
                        sem_r.at[d, a * 3 + e],
                    )
                )
    copies_t = [
        pltpu.make_async_copy(w_time_hbm.at[a + 1], wt.at[:, pl.ds(a * mid, mid)], sem_t.at[a])
        for a in range(2)
    ]
    copy_u = pltpu.make_async_copy(w_up_hbm, wu_raw, sem_u)
    for copy in copies_r + copies_t:
        copy.start()
    copy_u.start()

    taps = jnp.concatenate([w_in_ref[2 * one :], w_in_ref[one : 2 * one]], axis=0)
    w_in[...] = jnp.transpose(taps)
    c_in[...] = column(b_in_ref)
    c_gain[...] = column(gain_ref)
    c_res[...] = column(b_res_ref)
    c_time[...] = column(b_time_ref)
    c_up[...] = column(b_up_ref)
    src = lax.broadcasted_iota(jnp.int32, (2 * cols, 2 * cols), 0)
    dst = lax.broadcasted_iota(jnp.int32, (2 * cols, 2 * cols), 1)
    perm[...] = jnp.where(
        (src % cols == dst // 2) & (src // cols == dst % 2), 1.0, 0.0
    ).astype(BF16)

    n_frames, n_rows, n_cols = frames_ref[g], heights_ref[g], widths_ref[g]
    lane = lax.broadcasted_iota(jnp.int32, (1, cols), 1)

    def mask(f, r):
        live = (f < n_frames) & (r >= 0) & (r < n_rows)
        return lane < jnp.where(live, n_cols, 0)

    def mask2(f, r):
        return jnp.concatenate([mask(f, r), mask(f, r + 1)], axis=1)

    def wide(ref):
        return jnp.concatenate([ref[...], ref[...]], axis=1)

    for f in range(LFRAMES):
        base = (1 - f) * one
        for q in range(rows + 6):
            x = grid_ref[f, q].astype(F32)
            x = jnp.where(mask(f, rows * t - 3 + q), x, 0.0)
            for e, y in enumerate((shift(x, 1), x, shift(x, -1))):
                y = y.astype(BF16)
                for d in range(3):
                    if 0 <= q - d < mrows:
                        at = base + (d * 3 + e) * channels
                        x_in[at : at + channels, (q - d) * cols : (q - d + 1) * cols] = y

    def stage_first(p, carry):
        at = pl.multiple_of(p * 2 * cols, 2 * cols)
        for f in range(LFRAMES):
            if f == 0:
                acc = jnp.dot(
                    w_in[:, 0:one],
                    x_in[one : 2 * one, pl.ds(at, 2 * cols)],
                    preferred_element_type=F32,
                )
            else:
                acc = jnp.dot(
                    w_in[...], x_in[:, pl.ds(at, 2 * cols)], preferred_element_type=F32
                )
            half = (acc + wide(c_in)).astype(BF16)
            first[f, :, pl.ds(at, 2 * cols)] = half
            v = half.astype(F32)
            mean = jnp.sum(v * v, axis=0, keepdims=True) * (1.0 / mid)
            v = v * lax.rsqrt(mean + 1e-06) * wide(c_gain)
            v = v / (1.0 + jnp.exp(-v))
            v = jnp.where(mask2(f, rows * t - 2 + 2 * p), v, 0.0)
            for e in range(3):
                parts = [v[:, i * cols : (i + 1) * cols] for i in range(2)]
                if e != 1:
                    parts = [shift(part, 1 - e) for part in parts]
                spread[
                    (f * 3 + e) * mid : (f * 3 + e + 1) * mid, pl.ds(at, 2 * cols)
                ] = jnp.concatenate(parts, axis=1).astype(BF16)
        return carry

    lax.fori_loop(0, mrows // 2, stage_first, 0)

    for copy in copies_r:
        copy.wait()
    for copy in copies_t:
        copy.wait()

    def stage_block(p, carry):
        at = pl.multiple_of(p * 2 * cols, 2 * cols)
        here = pl.ds(pl.multiple_of(at + cols, cols), 2 * cols)
        accs = [first[f, :, here].astype(F32) + wide(c_res) for f in range(LFRAMES)]
        for d in range(3):
            there = pl.ds(pl.multiple_of(at + d * cols, cols), 2 * cols)
            accs[0] = accs[0] + jnp.dot(
                wr[d, :, 3 * mid :], spread[0 : 3 * mid, there], preferred_element_type=F32
            )
            accs[1] = accs[1] + jnp.dot(
                wr[d], spread[:, there], preferred_element_type=F32
            )
        blocks = [acc.astype(BF16) for acc in accs]
        both = jnp.concatenate(blocks, axis=0)
        for f in range(LFRAMES):
            if f == 0:
                twice = jnp.dot(wt[:, mid:], blocks[0], preferred_element_type=F32)
            else:
                twice = jnp.dot(wt[...], both, preferred_element_type=F32)
            twice = jnp.where(mask2(f, rows * t - 1 + 2 * p), twice + wide(c_time), 0.0)
            twice = twice.astype(BF16)
            for k in range(2):
                timed[2 * f + k, :, pl.ds(at, 2 * cols)] = twice[k * mid : (k + 1) * mid]
        return carry

    lax.fori_loop(0, (rows + 2) // 2, stage_block, 0)

    copy_u.wait()
    w0, w1, w2 = [wu_raw[d].reshape(3 * outc, mid) for d in range(3)]
    wu[0, :, 0:mid] = w0
    wu[0, :, mid:] = (w1.astype(F32) + w2.astype(F32)).astype(BF16)
    wu[1, :, 0:mid] = (w0.astype(F32) + w1.astype(F32)).astype(BF16)
    wu[1, :, mid:] = w2

    def stage_up(f, carry):
        for p in range(rows // 2):
            x = [timed[f, :, (2 * p + i) * cols : (2 * p + i + 2) * cols] for i in range(3)]
            for k in range(2):
                z = jnp.dot(
                    wu[k],
                    jnp.concatenate([x[k], x[k + 1]], axis=0),
                    preferred_element_type=F32,
                )
                for i in range(2):
                    r = 2 * p + i
                    z0, z1, z2 = [
                        z[e * outc : (e + 1) * outc, i * cols : (i + 1) * cols] for e in range(3)
                    ]
                    live = mask(f // 2, rows * t + r)
                    base = z1 + c_up[...]
                    even = jnp.where(live, shift(z0, 1) + z2 + base, 0.0)
                    odd = jnp.where(live, z0 + shift(z2, -1) + base, 0.0)
                    pair = jnp.concatenate([even, odd], axis=1).astype(BF16)
                    row = jnp.dot(pair, perm[...], preferred_element_type=F32)
                    for w in range(2):
                        inter[w, pl.ds(2 * r + k, outc, stride=2 * rows), :] = row[
                            :, w * cols : (w + 1) * cols
                        ]
        for w in range(2):
            out_ref[0, :, f, :, w * cols : (w + 1) * cols] = (
                inter[w].reshape(outc, 2 * rows, cols).astype(BF16)
            )
        return carry

    lax.fori_loop(0, 2 * LFRAMES, stage_up, 0)


def decode(grid, frames, heights, widths, w_in, biases, w_res, w_time, w_up):
    rows, cols = grid.shape[1] - 6, grid.shape[3]
    channels = grid.shape[2]
    mid, outc = w_res.shape[3], w_up.shape[2]
    smem = pl.BlockSpec(memory_space=pltpu.SMEM)
    vmem = pl.BlockSpec(memory_space=pltpu.VMEM)
    anywhere = pl.BlockSpec(memory_space=pl.ANY)
    return pl.pallas_call(
        decode_kernel,
        out_shape=jax.ShapeDtypeStruct((1, outc, 2 * LFRAMES, 2 * rows, 2 * cols), BF16),
        in_specs=[smem] * 3 + [vmem] * 7 + [anywhere] * 3,
        out_specs=vmem,
        scratch_shapes=[
            pltpu.VMEM((mid, 18 * channels), BF16),
            pltpu.VMEM((3, mid, 6 * mid), BF16),
            pltpu.VMEM((2 * mid, 2 * mid), BF16),
            pltpu.VMEM(w_up.shape, BF16),
            pltpu.VMEM((2, 3 * outc, 2 * mid), BF16),
            pltpu.VMEM((18 * channels, (rows + 4) * cols), BF16),
            pltpu.VMEM((LFRAMES, mid, (rows + 4) * cols), BF16),
            pltpu.VMEM((6 * mid, (rows + 4) * cols), BF16),
            pltpu.VMEM((2 * LFRAMES, mid, (rows + 2) * cols), BF16),
            pltpu.VMEM((2, outc * 2 * rows, cols), F32),
            pltpu.VMEM((2 * cols, 2 * cols), BF16),
            pltpu.VMEM((mid, 128), F32),
            pltpu.VMEM((mid, 128), F32),
            pltpu.VMEM((mid, 128), F32),
            pltpu.VMEM((2 * mid, 128), F32),
            pltpu.VMEM((outc, 128), F32),
            pltpu.SemaphoreType.DMA((3, 6)),
            pltpu.SemaphoreType.DMA((2,)),
            pltpu.SemaphoreType.DMA,
        ],
        compiler_params=pltpu.CompilerParams(vmem_limit_bytes=48 * 2**20),
        name="decode",
    )(frames, heights, widths, grid, w_in, *biases, w_res, w_time, w_up)


def solution(mesh):
    n_req, n_tile = mesh.shape["req"], mesh.shape["tile"]

    def on_device(
        latents, piece_dest, frames, heights, widths,
        w_in, b_in, gain_norm, w_res, b_res, w_time, b_time, w_up, b_up,
    ):
        grid = route(n_req, n_tile, piece_dest, latents)
        mid, channels = w_in.shape[3], w_in.shape[4]
        taps = jnp.transpose(w_in, (0, 1, 2, 4, 3)).reshape(27 * channels, mid)
        biases = [b.reshape(1, -1) for b in (b_in, gain_norm, b_res, b_time, b_up)]
        return decode(grid, frames, heights, widths, taps, biases, w_res, w_time, w_up)

    return jax.shard_map(
        on_device,
        mesh=mesh,
        in_specs=(P(("req", "tile"), None, None),) + (P(),) * 13,
        out_specs=P("req", None, None, "tile", None),
        check_vma=False,
    )
```

time: 270 us -> 56 us (0.21)
  matrix products: 68.5 us -> 0 us
  local copies, waits for them, and re-layouts: 77 us -> 10.6 us
  waiting for transfers between devices: 63.8 us -> 0 us
  Pallas kernels: 0 us -> 44.7 us
  other arithmetic: 31 us -> 0 us
  between operations: 14 us -> 0.03 us
  starting transfers between devices: 13.9 us -> 0 us
    dot_general x25 -> x0, matrix products: 68.5 us -> none  [the longest x3 33.1 us: on_device(): jnp.einsum('okc,kcthw->othw', kernel, shifted[:, :, :, tap_r:tap_r + out_...]
    all_gather x1 -> x0, waiting for transfers between devices: 52.7 us -> none  [on_device(): lax.all_gather(flattened, ('req', 'tile'), axis=0, tiled=True)]
    pallas_call x0 -> x2, Pallas kernels: none -> 44.7 us  [the longest x1 29.5 us: decode(): pl.pallas_call(decode_kernel, out_shape=jax.ShapeDtypeStruct((1, outc, 2...]
    another operation x6 -> x0, local copies, waits for them, and re-layouts: 31.9 us -> none  [the longest x2 27.4 us: on_device(): jnp.stack([padded[..., tap_c:tap_c + out_cols] for tap_c in range(3)], ax...]
    another operation x3 -> x0, other arithmetic: 22.7 us -> none  [the longest x1 19.8 us: on_device(): jnp.stack([padded[..., tap_c:tap_c + out_cols] for tap_c in range(3)], ax...]
    ppermute x6 -> x0, starting transfers between devices: 13.9 us -> none  [the longest x3 7.21 us: with_halo(): lax.ppermute(tail, axis, [(i, (i + 1) % count) for i in range(ends)])]
    ppermute x6 -> x0, waiting for transfers between devices: 11.1 us -> none  [the longest x3 9.62 us: with_halo(): lax.ppermute(head, axis, [((i + 1) % count, i) for i in range(ends)])]
    slice x6 -> x0, local copies, waits for them, and re-layouts: 10.8 us -> none  [the longest x1 8.36 us: causal_conv(): shifted[:, :, tap_t:tap_t + frame_count, tap_r:tap_r + row_count, :]]
  transfers between devices with their start and end apart: 7 -> 0, of which waited for: 5 -> 0; matrix products, arithmetic and copies ran while one was open for 3% -> 0% of each run, Pallas kernels for 0% -> 0%
where the time goes in v1:
time: 56 us; the launch traced here: 55.3 us
  Pallas kernels  44.7 us (80%)
  local copies, waits for them, and re-layouts  10.6 us (19%)
    pallas_call x1, Pallas kernels, decode(): pl.pallas_call(decode_kernel, out_shape=jax.ShapeDtypeStruct((1, outc, 2...  29.5 us
    pallas_call x1, Pallas kernels, route(): pl.pallas_call(functools.partial(route_kernel, n_req, n_tile), out_shape=...  15.2 us
    unnamed x18, local copies, waits for them, and re-layouts  7.85 us
    reshape x4, local copies, waits for them, and re-layouts, on_device(): biases = [b.reshape(1, -1) for b in (b_in, gain_norm, b_res, b_time, b_up)]  2.74 us

profile of v1, /device:TPU:1, one launch (start us, length us, event | category | flops | bytes accessed | tf_op | source)
XLA Modules:
  0.0 55.3 jit_solution(14738895113948276306)
XLA Ops:
  0.0 0.7 %reshape.19.b_in_ref = f32[1,384]{1,0:T(1,128)S(1)} reshape(f32[384]{0:T(512)} %param.20) | data formatting | bytes 3072 | tf_op jit(solution)/shard_map/reshape | solution.py:450
  0.7 0.7 %reshape.20.gain_ref = f32[1,384]{1,0:T(1,128)S(1)} reshape(f32[384]{0:T(512)} %param.21) | data formatting | bytes 3072 | tf_op jit(solution)/shard_map/reshape | solution.py:450
  1.4 0.7 %reshape.21.b_res_ref = f32[1,384]{1,0:T(1,128)S(1)} reshape(f32[384]{0:T(512)} %param.23) | data formatting | bytes 3072 | tf_op jit(solution)/shard_map/reshape | solution.py:450
  2.0 0.7 %reshape.22.b_time_ref = f32[1,768]{1,0:T(1,128)S(1)} reshape(f32[768]{0:T(1024)} %param.25) | data formatting | bytes 6144 | tf_op jit(solution)/shard_map/reshape | solution.py:450
  2.7 0.0 copy-start.3
  2.7 0.8 %copy-done.3 = bf16[8,16,128]{2,1,0:T(8,128)(2,1)S(1)} copy-done((bf16[8,16,128]{2,1,0:T(8,128)(2,1)S(1)}, bf16[8,16,128]{2,1,0:T(8,128)(2,1)}, u32[]{:S(2)}) %copy-start.3) | copy-done | bytes 32792
  3.5 0.0 copy-start.4
  3.5 0.7 %copy-done.4 = s32[256]{0:T(256)S(1)} copy-done((s32[256]{0:T(256)S(1)}, s32[256]{0:T(256)}, u32[]{:S(2)}) %copy-start.4) | copy-done | bytes 1048
  4.2 15.2 %route.1.grid_ref = bf16[2,10,16,128]{3,2,1,0:T(8,128)(2,1)S(1)} custom-call(s32[256]{0:T(256)S(1)} %copy-done.4, bf16[8,16,128]{2,1,0:T(8,128)(2,1)S(1)} %copy-done.3), custom_call_target="tpu_custom_call" | custom-call | tf_op jit(solution)/shard_map/route/pallas_call | solution.py:160
  19.3 0.0 copy-start
  19.4 1.5 %copy-done = bf16[3,768,384]{2,1,0:T(8,128)(2,1)S(1)} copy-done((bf16[3,768,384]{2,1,0:T(8,128)(2,1)S(1)}, bf16[3,768,384]{2,1,0:T(8,128)(2,1)}, u32[]{:S(2)}) %copy-start) | copy-done | bytes 1769496
  20.8 0.0 copy-start.1
  20.8 1.3 %copy-done.1 = bf16[3,3,192,384]{3,2,1,0:T(8,128)(2,1)S(1)} copy-done((bf16[3,3,192,384]{3,2,1,0:T(8,128)(2,1)S(1)}, bf16[3,3,192,384]{3,2,1,0:T(8,128)(2,1)}, u32[]{:S(2)}) %copy-start.1) | copy-done | bytes 1327128
  22.1 0.0 copy-start.2
  22.2 1.0 %copy-done.2 = bf16[3,3,3,384,16]{3,4,2,1,0:T(8,128)(2,1)S(1)} copy-done((bf16[3,3,3,384,16]{3,4,2,1,0:T(8,128)(2,1)S(1)}, bf16[3,3,3,384,16]{3,4,2,1,0:T(8,128)(2,1)}, u32[]{:S(2)}) %copy-start.2) | copy-done | bytes 331800
  23.1 0.0 copy-start.5
  23.1 0.7 %copy-done.5 = f32[192]{0:T(256)S(1)} copy-done((f32[192]{0:T(256)S(1)}, f32[192]{0:T(256)}, u32[]{:S(2)}) %copy-start.5) | copy-done | bytes 792
  23.8 0.0 copy-start.6
  23.8 0.7 %copy-done.6 = s32[8]{0:T(128)S(1)} copy-done((s32[8]{0:T(128)S(1)}, s32[8]{0:T(128)}, u32[]{:S(2)}) %copy-start.6) | copy-done | bytes 56
  24.5 0.0 copy-start.7
  24.5 0.7 %copy-done.7 = s32[8]{0:T(128)S(1)} copy-done((s32[8]{0:T(128)S(1)}, s32[8]{0:T(128)}, u32[]{:S(2)}) %copy-start.7) | copy-done | bytes 56
  25.1 0.0 copy-start.8
  25.1 0.7 %copy-done.8 = s32[8]{0:T(128)S(1)} copy-done((s32[8]{0:T(128)S(1)}, s32[8]{0:T(128)}, u32[]{:S(2)}) %copy-start.8) | copy-done | bytes 56
  25.8 29.5 %decode.1 = bf16[1,192,4,8,256]{4,3,2,1,0:T(8,128)(2,1)} custom-call(s32[8]{0:T(128)S(1)} %copy-done.6, s32[8]{0:T(128)S(1)} %copy-done.7, s32[8]{0:T(128)S(1)} %copy-done.8, bf16[2,10,16,128]{3,2,1,0:T(8,128)(2,1)S(1)} %route.1.grid_ref, bf16[432,384]{1,0:T(8,128)(2,1)S(1)} %bitcast.4, f32[1,384]{1,0:T(1,128)S(1)} %reshape.19.b_in_ref, ...), custom_call_target="tpu_custom_call" | custom-call | tf_op jit(solution)/shard_map/decode/pallas_call | solution.py:409
Async XLA Ops:
  2.7 0.8 %copy-start.3 = (bf16[8,16,128]{2,1,0:T(8,128)(2,1)S(1)}, bf16[8,16,128]{2,1,0:T(8,128)(2,1)}, u32[]{:S(2)}) copy-start(bf16[8,16,128]{2,1,0:T(8,128)(2,1)} %lat_ref.1) | copy-start | bytes 98308
  3.5 0.7 %copy-start.4 = (s32[256]{0:T(256)S(1)}, s32[256]{0:T(256)}, u32[]{:S(2)}) copy-start(s32[256]{0:T(256)} %dest_ref.1) | copy-start | bytes 3076
  19.3 1.5 %copy-start = (bf16[3,768,384]{2,1,0:T(8,128)(2,1)S(1)}, bf16[3,768,384]{2,1,0:T(8,128)(2,1)}, u32[]{:S(2)}) copy-start(bf16[3,768,384]{2,1,0:T(8,128)(2,1)} %w_time_hbm.1) | copy-start | bytes 5308420
  20.8 1.3 %copy-start.1 = (bf16[3,3,192,384]{3,2,1,0:T(8,128)(2,1)S(1)}, bf16[3,3,192,384]{3,2,1,0:T(8,128)(2,1)}, u32[]{:S(2)}) copy-start(bf16[3,3,192,384]{3,2,1,0:T(8,128)(2,1)} %w_up_hbm.1) | copy-start | bytes 3981316
  22.1 1.0 %copy-start.2 = (bf16[3,3,3,384,16]{3,4,2,1,0:T(8,128)(2,1)S(1)}, bf16[3,3,3,384,16]{3,4,2,1,0:T(8,128)(2,1)}, u32[]{:S(2)}) copy-start(bf16[3,3,3,384,16]{3,4,2,1,0:T(8,128)(2,1)} %param.19) | copy-start | bytes 995332
  23.1 0.7 %copy-start.5 = (f32[192]{0:T(256)S(1)}, f32[192]{0:T(256)}, u32[]{:S(2)}) copy-start(f32[192]{0:T(256)} %param.27) | copy-start | bytes 2308
  23.8 0.7 %copy-start.6 = (s32[8]{0:T(128)S(1)}, s32[8]{0:T(128)}, u32[]{:S(2)}) copy-start(s32[8]{0:T(128)} %frames_ref.1) | copy-start | bytes 100
  24.5 0.7 %copy-start.7 = (s32[8]{0:T(128)S(1)}, s32[8]{0:T(128)}, u32[]{:S(2)}) copy-start(s32[8]{0:T(128)} %heights_ref.1) | copy-start | bytes 100
  25.1 0.7 %copy-start.8 = (s32[8]{0:T(128)S(1)}, s32[8]{0:T(128)}, u32[]{:S(2)}) copy-start(s32[8]{0:T(128)} %widths_ref.1) | copy-start | bytes 100

commit v2 on v1

v2 whole, which is shorter than its diff:
```python
import functools

import jax
import jax.numpy as jnp
from jax import lax
from jax.experimental import pallas as pl
from jax.experimental.pallas import tpu as pltpu
from jax.sharding import PartitionSpec as P

LFRAMES = 2
MESH = pl.DeviceIdType.MESH
VMEM_BYTES = 63 * 2**20
F32 = jnp.float32
BF16 = jnp.bfloat16


def route_kernel(
    n_req, n_tile, dest_hbm, lat_ref, out_ref,
    dest_ref, buf, sel, dest_sem, send_sem, recv_sem, side_send, side_recv,
):
    g = lax.axis_index("req")
    t = lax.axis_index("tile")
    half = n_tile // 2
    slots = lat_ref.shape[0]
    rows = slots // LFRAMES

    fetch = pltpu.make_async_copy(dest_hbm, dest_ref, dest_sem)
    fetch.start()
    barrier = pltpu.get_barrier_semaphore()

    def greet(k, carry):
        other = lax.rem(g + k, n_req)
        for f in range(LFRAMES):
            source = f * half + t // 2

            @pl.when((k > 0) | (source != t))
            def _():
                pl.semaphore_signal(
                    barrier, inc=1, device_id=(other, source), device_id_type=MESH
                )

        return carry

    lax.fori_loop(0, n_req, greet, 0)

    @pl.when(t > 0)
    def _():
        pl.semaphore_signal(barrier, inc=1, device_id=(g, t - 1), device_id_type=MESH)

    @pl.when(t < n_tile - 1)
    def _():
        pl.semaphore_signal(barrier, inc=1, device_id=(g, t + 1), device_id_type=MESH)

    inner = (t + n_tile - 1) // n_tile - (t + 1) // n_tile
    pl.semaphore_wait(barrier, 2 * n_req + 2 * inner)

    frame = t // half
    first_tile = 2 * lax.rem(t, half)

    def remote(k, h):
        return pltpu.make_async_remote_copy(
            src_ref=lat_ref.at[pl.ds(h * rows, rows)],
            dst_ref=buf.at[g, frame],
            send_sem=send_sem.at[k, h],
            recv_sem=recv_sem.at[g, frame],
            device_id=(lax.rem(g + k, n_req), first_tile + h),
            device_id_type=MESH,
        )

    def local(h):
        return pltpu.make_async_copy(
            lat_ref.at[pl.ds(h * rows, rows)], buf.at[g, frame], recv_sem.at[g, frame]
        )

    def send(k, carry):
        for h in range(2):

            @pl.when((k > 0) | (first_tile + h != t))
            def _():
                remote(k, h).start()

            @pl.when((k == 0) & (first_tile + h == t))
            def _():
                local(h).start()

        return carry

    lax.fori_loop(0, n_req, send, 0)

    def arrive(s, carry):
        for f in range(LFRAMES):
            pltpu.make_async_copy(buf.at[s, f], buf.at[s, f], recv_sem.at[s, f]).wait()
        return carry

    lax.fori_loop(0, n_req, arrive, 0)

    fetch.wait()
    per = slots * n_tile
    source = jnp.int32(0)
    for j in range(n_req):
        source = jnp.where(dest_ref[j * per] // per == g, j, source)
    sel[:, 3 : 3 + rows] = buf[source]

    up = pltpu.make_async_remote_copy(
        src_ref=sel.at[:, pl.ds(3, 3)],
        dst_ref=sel.at[:, pl.ds(3 + rows, 3)],
        send_sem=side_send.at[0],
        recv_sem=side_recv.at[0],
        device_id=(g, t - 1),
        device_id_type=MESH,
    )
    down = pltpu.make_async_remote_copy(
        src_ref=sel.at[:, pl.ds(rows, 3)],
        dst_ref=sel.at[:, pl.ds(0, 3)],
        send_sem=side_send.at[1],
        recv_sem=side_recv.at[1],
        device_id=(g, t + 1),
        device_id_type=MESH,
    )
    zeros = jnp.zeros((LFRAMES, 3) + lat_ref.shape[1:], BF16)

    @pl.when(t > 0)
    def _():
        up.start()

    @pl.when(t < n_tile - 1)
    def _():
        down.start()

    @pl.when(t == 0)
    def _():
        sel[:, 0:3] = zeros

    @pl.when(t == n_tile - 1)
    def _():
        sel[:, 3 + rows :] = zeros

    def sent(k, carry):
        for h in range(2):

            @pl.when((k > 0) | (first_tile + h != t))
            def _():
                remote(k, h).wait_send()

        return carry

    lax.fori_loop(0, n_req, sent, 0)

    @pl.when(t > 0)
    def _():
        up.wait_send()
        down.wait_recv()

    @pl.when(t < n_tile - 1)
    def _():
        down.wait_send()
        up.wait_recv()

    out_ref[...] = sel[...]


def route(n_req, n_tile, piece_dest, latents):
    slots, channels, cols = latents.shape
    rows = slots // LFRAMES
    return pl.pallas_call(
        functools.partial(route_kernel, n_req, n_tile),
        out_shape=jax.ShapeDtypeStruct((LFRAMES, rows + 6, channels, cols), BF16),
        in_specs=[pl.BlockSpec(memory_space=pltpu.HBM)] * 2,
        out_specs=pl.BlockSpec(memory_space=pltpu.VMEM),
        scratch_shapes=[
            pltpu.SMEM(piece_dest.shape, jnp.int32),
            pltpu.VMEM((n_req, LFRAMES, rows, channels, cols), BF16),
            pltpu.VMEM((LFRAMES, rows + 6, channels, cols), BF16),
            pltpu.SemaphoreType.DMA,
            pltpu.SemaphoreType.DMA((n_req, 2)),
            pltpu.SemaphoreType.DMA((n_req, LFRAMES)),
            pltpu.SemaphoreType.DMA((2,)),
            pltpu.SemaphoreType.DMA((2,)),
        ],
        compiler_params=pltpu.CompilerParams(
            collective_id=0, has_side_effects=True, vmem_limit_bytes=VMEM_BYTES
        ),
        name="route",
    )(piece_dest, latents)


def shift(x, by):
    width = x.shape[1]
    lane = lax.broadcasted_iota(jnp.int32, x.shape, 1)
    if by == 1:
        return jnp.where(lane == 0, 0.0, pltpu.roll(x, 1, axis=1))
    return jnp.where(lane == width - 1, 0.0, pltpu.roll(x, width - 1, axis=1))


def column(ref):
    n = ref.shape[0]
    return jnp.transpose(jnp.broadcast_to(ref[...].reshape(1, n), (128, n)))


def decode_kernel(grid_ref, *refs):
    hbm, (out_ref, *refs) = refs[:12], refs[12:]
    frames_hbm, heights_hbm, widths_hbm, w_in_hbm = hbm[:4]
    vector_hbm, (w_res_hbm, w_time_hbm, w_up_hbm) = hbm[4:9], hbm[9:]
    frames_ref, heights_ref, widths_ref, *refs = refs
    vectors, refs = refs[:5], refs[5:]
    taps, w_in, wr, wt, wu_raw, wu, x_in, first, spread, timed, inter, perm, *refs = refs
    c_in, c_gain, c_res, c_time, c_up, sem_s, sem_v, sem_i, sem_r, sem_t, sem_u = refs
    g = lax.axis_index("req")
    t = lax.axis_index("tile")
    channels, cols = grid_ref.shape[2], grid_ref.shape[3]
    rows = grid_ref.shape[1] - 6
    mid = taps.shape[1]
    outc = wu_raw.shape[2]
    one = 9 * channels
    mrows = rows + 4

    copies_s = [
        pltpu.make_async_copy(a, b, sem_s.at[i])
        for i, (a, b) in enumerate(
            zip((frames_hbm, heights_hbm, widths_hbm), (frames_ref, heights_ref, widths_ref))
        )
    ]
    copies_v = [
        pltpu.make_async_copy(a, b, sem_v.at[i])
        for i, (a, b) in enumerate(zip(vector_hbm, vectors))
    ]
    copies_i = [
        pltpu.make_async_copy(
            w_in_hbm.at[pl.ds((2 - i) * one, one)], taps.at[pl.ds(i * one, one)], sem_i.at[i]
        )
        for i in range(2)
    ]
    copies_r = []
    for d in range(3):
        for a in range(2):
            for e in range(3):
                copies_r.append(
                    pltpu.make_async_copy(
                        w_res_hbm.at[2 - a, d, e],
                        wr.at[pl.ds(a * mid, mid), pl.ds((d * 3 + e) * mid, mid)],
                        sem_r.at[d, a * 3 + e],
                    )
                )
    copies_t = [
        pltpu.make_async_copy(w_time_hbm.at[a + 1], wt.at[:, pl.ds(a * mid, mid)], sem_t.at[a])
        for a in range(2)
    ]
    copy_u = pltpu.make_async_copy(w_up_hbm, wu_raw, sem_u)
    for copy in copies_s + copies_v + copies_i + copies_r + copies_t + [copy_u]:
        copy.start()

    for copy in copies_s + copies_v + copies_i:
        copy.wait()
    w_in[...] = jnp.transpose(taps[...])
    for kept, vector in zip((c_in, c_gain, c_res, c_time, c_up), vectors):
        kept[...] = column(vector)
    src = lax.broadcasted_iota(jnp.int32, (2 * cols, 2 * cols), 0)
    dst = lax.broadcasted_iota(jnp.int32, (2 * cols, 2 * cols), 1)
    perm[...] = jnp.where(
        (src % cols == dst // 2) & (src // cols == dst % 2), 1.0, 0.0
    ).astype(BF16)

    n_frames, n_rows, n_cols = frames_ref[g], heights_ref[g], widths_ref[g]
    lane = lax.broadcasted_iota(jnp.int32, (1, cols), 1)

    def mask(f, r):
        live = (f < n_frames) & (r >= 0) & (r < n_rows)
        return lane < jnp.where(live, n_cols, 0)

    def masks(f, r, n):
        return jnp.concatenate([mask(f, r + i) for i in range(n)], axis=1)

    def wide(ref, n):
        return jnp.concatenate([ref[...]] * n, axis=1)

    for f in range(LFRAMES):
        base = (1 - f) * one
        for q in range(rows + 6):
            x = grid_ref[f, q].astype(F32)
            x = jnp.where(mask(f, rows * t - 3 + q), x, 0.0)
            for e, y in enumerate((shift(x, 1), x, shift(x, -1))):
                y = y.astype(BF16)
                for d in range(3):
                    if 0 <= q - d < mrows:
                        at = base + (d * 3 + e) * channels
                        x_in[at : at + channels, (q - d) * cols : (q - d + 1) * cols] = y

    span = mrows // 2

    def stage_first(p, carry):
        at = pl.multiple_of(p * span * cols, span * cols)
        here = pl.ds(at, span * cols)
        for f in range(LFRAMES):
            if f == 0:
                x = x_in[one : 2 * one, here]
            else:
                x = x_in[:, here]
            acc = jnp.dot(w_in[:, 0 : x.shape[0]], x, preferred_element_type=F32)
            half = (acc + wide(c_in, span)).astype(BF16)
            first[f, :, here] = half
            v = half.astype(F32)
            mean = jnp.sum(v * v, axis=0, keepdims=True) * (1.0 / mid)
            v = v * lax.rsqrt(mean + 1e-06) * wide(c_gain, span)
            v = v / (1.0 + jnp.exp(-v))
            v = jnp.where(masks(f, rows * t - 2 + span * p, span), v, 0.0)
            parts = [v[:, i * cols : (i + 1) * cols] for i in range(span)]
            for e in range(3):
                moved = parts if e == 1 else [shift(part, 1 - e) for part in parts]
                spread[(f * 3 + e) * mid : (f * 3 + e + 1) * mid, here] = jnp.concatenate(
                    moved, axis=1
                ).astype(BF16)
        return carry

    lax.fori_loop(0, 2, stage_first, 0)

    for copy in copies_r + copies_t:
        copy.wait()

    brows = rows + 2
    taller = [
        jnp.concatenate(
            [
                spread[f * 3 * mid : (f + 1) * 3 * mid, d * cols : (d + brows) * cols]
                for d in range(3)
            ],
            axis=0,
        )
        for f in range(LFRAMES)
    ]
    old = jnp.dot(wr[...], taller[0], preferred_element_type=F32)
    new = jnp.dot(wr[0:mid], taller[1], preferred_element_type=F32)
    blocks = []
    for f, acc in enumerate((old[0:mid], old[mid:] + new)):
        kept = first[f, :, cols : (brows + 1) * cols].astype(F32)
        blocks.append((acc + wide(c_res, brows) + kept).astype(BF16))
    for f in range(LFRAMES):
        if f == 0:
            twice = jnp.dot(wt[:, mid:], blocks[0], preferred_element_type=F32)
        else:
            both = jnp.concatenate(blocks, axis=0)
            twice = jnp.dot(wt[...], both, preferred_element_type=F32)
        live = masks(f, rows * t - 1, brows)
        twice = jnp.where(live, twice + wide(c_time, brows), 0.0).astype(BF16)
        for k in range(2):
            timed[2 * f + k] = twice[k * mid : (k + 1) * mid]

    copy_u.wait()
    w0, w1, w2 = [wu_raw[d].reshape(3 * outc, mid) for d in range(3)]
    wu[0, :, 0:mid] = w0
    wu[0, :, mid:] = (w1.astype(F32) + w2.astype(F32)).astype(BF16)
    wu[1, :, 0:mid] = (w0.astype(F32) + w1.astype(F32)).astype(BF16)
    wu[1, :, mid:] = w2

    def stage_up(f, carry):
        x = [timed[f, :, i * cols : (i + rows) * cols] for i in range(3)]
        for k in range(2):
            z = jnp.dot(
                wu[k],
                jnp.concatenate([x[k], x[k + 1]], axis=0),
                preferred_element_type=F32,
            )
            for r in range(rows):
                z0, z1, z2 = [
                    z[e * outc : (e + 1) * outc, r * cols : (r + 1) * cols] for e in range(3)
                ]
                live = mask(f // 2, rows * t + r)
                base = z1 + c_up[...]
                even = jnp.where(live, shift(z0, 1) + z2 + base, 0.0)
                odd = jnp.where(live, z0 + shift(z2, -1) + base, 0.0)
                pair = jnp.concatenate([even, odd], axis=1).astype(BF16)
                row = jnp.dot(pair, perm[...], preferred_element_type=F32)
                for w in range(2):
                    inter[w, pl.ds(2 * r + k, outc, stride=2 * rows), :] = row[
                        :, w * cols : (w + 1) * cols
                    ]
        for w in range(2):
            out_ref[0, :, f, :, w * cols : (w + 1) * cols] = (
                inter[w].reshape(outc, 2 * rows, cols).astype(BF16)
            )
        return carry

    lax.fori_loop(0, 2 * LFRAMES, stage_up, 0)


def decode(grid, frames, heights, widths, w_in, vectors, w_res, w_time, w_up):
    rows, cols = grid.shape[1] - 6, grid.shape[3]
    channels = grid.shape[2]
    mid, outc = w_res.shape[3], w_up.shape[2]
    vmem = pl.BlockSpec(memory_space=pltpu.VMEM)
    return pl.pallas_call(
        decode_kernel,
        out_shape=jax.ShapeDtypeStruct((1, outc, 2 * LFRAMES, 2 * rows, 2 * cols), BF16),
        in_specs=[vmem] + [pl.BlockSpec(memory_space=pltpu.HBM)] * 12,
        out_specs=vmem,
        scratch_shapes=[pltpu.SMEM(v.shape, jnp.int32) for v in (frames, heights, widths)]
        + [pltpu.VMEM(v.shape, F32) for v in vectors]
        + [
            pltpu.VMEM((18 * channels, mid), BF16),
            pltpu.VMEM((mid, 18 * channels), BF16),
            pltpu.VMEM((2 * mid, 9 * mid), BF16),
            pltpu.VMEM((2 * mid, 2 * mid), BF16),
            pltpu.VMEM(w_up.shape, BF16),
            pltpu.VMEM((2, 3 * outc, 2 * mid), BF16),
            pltpu.VMEM((18 * channels, (rows + 4) * cols), BF16),
            pltpu.VMEM((LFRAMES, mid, (rows + 4) * cols), BF16),
            pltpu.VMEM((6 * mid, (rows + 4) * cols), BF16),
            pltpu.VMEM((2 * LFRAMES, mid, (rows + 2) * cols), BF16),
            pltpu.VMEM((2, outc * 2 * rows, cols), F32),
            pltpu.VMEM((2 * cols, 2 * cols), BF16),
            pltpu.VMEM((mid, 128), F32),
            pltpu.VMEM((mid, 128), F32),
            pltpu.VMEM((mid, 128), F32),
            pltpu.VMEM((2 * mid, 128), F32),
            pltpu.VMEM((outc, 128), F32),
            pltpu.SemaphoreType.DMA((3,)),
            pltpu.SemaphoreType.DMA((5,)),
            pltpu.SemaphoreType.DMA((2,)),
            pltpu.SemaphoreType.DMA((3, 6)),
            pltpu.SemaphoreType.DMA((2,)),
            pltpu.SemaphoreType.DMA,
        ],
        compiler_params=pltpu.CompilerParams(vmem_limit_bytes=VMEM_BYTES),
        name="decode",
    )(grid, frames, heights, widths, w_in, *vectors, w_res, w_time, w_up)


def solution(mesh):
    n_req, n_tile = mesh.shape["req"], mesh.shape["tile"]

    def on_device(
        latents, piece_dest, frames, heights, widths,
        w_in, b_in, gain_norm, w_res, b_res, w_time, b_time, w_up, b_up,
    ):
        grid = route(n_req, n_tile, piece_dest, latents)
        mid, channels = w_in.shape[3], w_in.shape[4]
        taps = jnp.transpose(w_in, (0, 1, 2, 4, 3)).reshape(27 * channels, mid)
        vectors = (b_in, gain_norm, b_res, b_time, b_up)
        return decode(grid, frames, heights, widths, taps, vectors, w_res, w_time, w_up)

    return jax.shard_map(
        on_device,
        mesh=mesh,
        in_specs=(P(("req", "tile"), None, None),) + (P(),) * 13,
        out_specs=P("req", None, None, "tile", None),
        check_vma=False,
    )
```

time: 56 us -> 41.1 us (0.73)
  local copies, waits for them, and re-layouts: 10.6 us -> 0 us
  Pallas kernels: 44.7 us -> 40.7 us
    unnamed x18 -> x0, local copies, waits for them, and re-layouts: 7.85 us -> none
    pallas_call x1, Pallas kernels: 29.5 us -> 25.4 us  [decode(): pl.pallas_call(decode_kernel, out_shape=jax.ShapeDtypeStruct((1, outc, 2...]
    reshape x4 -> x0, local copies, waits for them, and re-layouts: 2.74 us -> none  [on_device(): biases = [b.reshape(1, -1) for b in (b_in, gain_norm, b_res, b_time, b_up)]]
where the time goes in v2:
time: 41.1 us; the launch traced here: 40.7 us
  Pallas kernels  40.7 us (99%)
    pallas_call x1, Pallas kernels, decode(): pl.pallas_call(decode_kernel, out_shape=jax.ShapeDtypeStruct((1, outc, 2...  25.4 us
    pallas_call x1, Pallas kernels, route(): pl.pallas_call(functools.partial(route_kernel, n_req, n_tile), out_shape=...  15.3 us

profile of v2, /device:TPU:1, one launch (start us, length us, event | category | flops | bytes accessed | tf_op | source)
XLA Modules:
  0.0 40.7 jit_solution(4983015278789133955)
XLA Ops:
  0.0 15.3 %route.1.grid_ref = bf16[2,10,16,128]{3,2,1,0:T(8,128)(2,1)} custom-call(s32[256]{0:T(256)} %dest_hbm.1, bf16[8,16,128]{2,1,0:T(8,128)(2,1)} %lat_ref.1), custom_call_target="tpu_custom_call" | custom-call | tf_op jit(solution)/shard_map/route/pallas_call | solution.py:165
  15.3 25.4 %decode.1 = bf16[1,192,4,8,256]{4,3,2,1,0:T(8,128)(2,1)} custom-call(bf16[2,10,16,128]{3,2,1,0:T(8,128)(2,1)} %route.1.grid_ref, s32[8]{0:T(128)} %refs_0_.1, s32[8]{0:T(128)} %refs_1_.1, s32[8]{0:T(128)} %refs_2_.1, bf16[432,384]{1,0:T(8,128)(2,1)} %bitcast.3, f32[384]{0:T(512)} %refs_4_.1, f32[384]{0:T(512)} %refs_5_.1, f32[384]{0:T(512)} %refs_6_.1, ...), custom_call_target="tpu_custom_call" | custom-call | tf_op jit(solution)/shard_map/decode/pallas_call | solution.py:390

commit v3 on v2

--- a/solution.py
+++ b/solution.py
@@ -16,152 +16,161 @@
 
 def route_kernel(
     n_req, n_tile, dest_hbm, lat_ref, out_ref,
-    dest_ref, buf, sel, dest_sem, send_sem, recv_sem, side_send, side_recv,
+    dest_ref, held, item, land, dest_sem, send_sem, recv_sem, send_two, recv_two,
 ):
     g = lax.axis_index("req")
     t = lax.axis_index("tile")
+    far = n_req // 2 if n_req < 8 else 4
+    low = n_req // far
+    line, place = g // low, lax.rem(g, low)
     half = n_tile // 2
     slots = lat_ref.shape[0]
     rows = slots // LFRAMES
+    has_up, has_down = t > 0, t < n_tile - 1
+    inner = (t + n_tile - 1) // n_tile - (t + 1) // n_tile
 
     fetch = pltpu.make_async_copy(dest_hbm, dest_ref, dest_sem)
     fetch.start()
     barrier = pltpu.get_barrier_semaphore()
 
-    def greet(k, carry):
-        other = lax.rem(g + k, n_req)
+    def greet(group, tile):
+        pl.semaphore_signal(barrier, inc=1, device_id=(group, tile), device_id_type=MESH)
+
+    def in_line(k):
+        return lax.rem(line + k, far) * low + place
+
+    def in_row(k):
+        return line * low + lax.rem(place + k, low)
+
+    for k in range(far):
         for f in range(LFRAMES):
             source = f * half + t // 2
-
-            @pl.when((k > 0) | (source != t))
-            def _():
-                pl.semaphore_signal(
-                    barrier, inc=1, device_id=(other, source), device_id_type=MESH
-                )
-
-        return carry
-
-    lax.fori_loop(0, n_req, greet, 0)
-
-    @pl.when(t > 0)
+            if k > 0:
+                greet(in_line(k), source)
+            else:
+                pl.when(source != t)(functools.partial(greet, g, source))
+    for k in range(low):
+        if k > 0:
+            greet(in_row(k), t)
+        pl.when(has_up)(functools.partial(greet, in_row(k), t - 1))
+        pl.when(has_down)(functools.partial(greet, in_row(k), t + 1))
+
+    zeros = jnp.zeros((low, LFRAMES, 3) + lat_ref.shape[1:], BF16)
+
+    @pl.when(t == 0)
     def _():
-        pl.semaphore_signal(barrier, inc=1, device_id=(g, t - 1), device_id_type=MESH)
-
-    @pl.when(t < n_tile - 1)
+        land[:, :, 0:3] = zeros
+
+    @pl.when(t == n_tile - 1)
     def _():
-        pl.semaphore_signal(barrier, inc=1, device_id=(g, t + 1), device_id_type=MESH)
-
-    inner = (t + n_tile - 1) // n_tile - (t + 1) // n_tile
-    pl.semaphore_wait(barrier, 2 * n_req + 2 * inner)
+        land[:, :, 3 + rows :] = zeros
+
+    pl.semaphore_wait(barrier, 2 * far - 1 + inner + low * (2 + inner) - 1)
 
     frame = t // half
     first_tile = 2 * lax.rem(t, half)
 
-    def remote(k, h):
+    def one(k, h):
         return pltpu.make_async_remote_copy(
             src_ref=lat_ref.at[pl.ds(h * rows, rows)],
-            dst_ref=buf.at[g, frame],
+            dst_ref=held.at[line, frame],
             send_sem=send_sem.at[k, h],
-            recv_sem=recv_sem.at[g, frame],
-            device_id=(lax.rem(g + k, n_req), first_tile + h),
+            recv_sem=recv_sem.at[line, frame],
+            device_id=(in_line(k), first_tile + h),
             device_id_type=MESH,
         )
 
-    def local(h):
+    def own(h):
         return pltpu.make_async_copy(
-            lat_ref.at[pl.ds(h * rows, rows)], buf.at[g, frame], recv_sem.at[g, frame]
-        )
-
-    def send(k, carry):
+            lat_ref.at[pl.ds(h * rows, rows)], held.at[line, frame], recv_sem.at[line, frame]
+        )
+
+    for k in list(range(1, far)) + [0]:
         for h in range(2):
-
-            @pl.when((k > 0) | (first_tile + h != t))
-            def _():
-                remote(k, h).start()
-
-            @pl.when((k == 0) & (first_tile + h == t))
-            def _():
-                local(h).start()
-
-        return carry
-
-    lax.fori_loop(0, n_req, send, 0)
-
-    def arrive(s, carry):
-        for f in range(LFRAMES):
-            pltpu.make_async_copy(buf.at[s, f], buf.at[s, f], recv_sem.at[s, f]).wait()
-        return carry
-
-    lax.fori_loop(0, n_req, arrive, 0)
+            if k > 0:
+                one(k, h).start()
+            else:
+                pl.when(first_tile + h != t)(lambda h=h: one(0, h).start())
+                pl.when(first_tile + h == t)(lambda h=h: own(h).start())
 
     fetch.wait()
     per = slots * n_tile
-    source = jnp.int32(0)
-    for j in range(n_req):
-        source = jnp.where(dest_ref[j * per] // per == g, j, source)
-    sel[:, 3 : 3 + rows] = buf[source]
-
-    up = pltpu.make_async_remote_copy(
-        src_ref=sel.at[:, pl.ds(3, 3)],
-        dst_ref=sel.at[:, pl.ds(3 + rows, 3)],
-        send_sem=side_send.at[0],
-        recv_sem=side_recv.at[0],
-        device_id=(g, t - 1),
-        device_id_type=MESH,
-    )
-    down = pltpu.make_async_remote_copy(
-        src_ref=sel.at[:, pl.ds(rows, 3)],
-        dst_ref=sel.at[:, pl.ds(0, 3)],
-        send_sem=side_send.at[1],
-        recv_sem=side_recv.at[1],
-        device_id=(g, t + 1),
-        device_id_type=MESH,
-    )
-    zeros = jnp.zeros((LFRAMES, 3) + lat_ref.shape[1:], BF16)
-
-    @pl.when(t > 0)
-    def _():
-        up.start()
-
-    @pl.when(t < n_tile - 1)
-    def _():
-        down.start()
-
-    @pl.when(t == 0)
-    def _():
-        sel[:, 0:3] = zeros
-
-    @pl.when(t == n_tile - 1)
-    def _():
-        sel[:, 3 + rows :] = zeros
-
-    def sent(k, carry):
+
+    def source_of(group):
+        found = jnp.int32(0)
+        for j in range(n_req):
+            found = jnp.where(dest_ref[j * per] // per == group, j, found)
+        return found
+
+    sources = [source_of(in_row(k)) for k in range(low)]
+
+    for s in range(far):
+        for f in range(LFRAMES):
+            pltpu.make_async_copy(held.at[s, f], held.at[s, f], recv_sem.at[s, f]).wait()
+
+    def two(k, n, src, dst, count, tile):
+        return pltpu.make_async_remote_copy(
+            src_ref=item.at[k, :, pl.ds(src, count)],
+            dst_ref=land.at[place, :, pl.ds(dst, count)],
+            send_sem=send_two.at[k, n],
+            recv_sem=recv_two.at[place, n],
+            device_id=(in_row(k), tile),
+            device_id_type=MESH,
+        )
+
+    def across(k):
+        return two(k, 0, 0, 3, rows, t)
+
+    def up(k):
+        return two(k, 1, 0, 3 + rows, 3, t - 1)
+
+    def down(k):
+        return two(k, 2, rows - 3, 0, 3, t + 1)
+
+    def keep():
+        return pltpu.make_async_copy(
+            item.at[0], land.at[place, :, pl.ds(3, rows)], recv_two.at[place, 0]
+        )
+
+    for k in list(range(1, low)) + [0]:
+        item[k] = held[sources[k] // low]
+        if k > 0:
+            across(k).start()
+        else:
+            keep().start()
+        pl.when(has_up)(lambda k=k: up(k).start())
+        pl.when(has_down)(lambda k=k: down(k).start())
+
+    for k in range(far):
         for h in range(2):
-
-            @pl.when((k > 0) | (first_tile + h != t))
-            def _():
-                remote(k, h).wait_send()
-
-        return carry
-
-    lax.fori_loop(0, n_req, sent, 0)
-
-    @pl.when(t > 0)
-    def _():
-        up.wait_send()
-        down.wait_recv()
-
-    @pl.when(t < n_tile - 1)
-    def _():
-        down.wait_send()
-        up.wait_recv()
-
-    out_ref[...] = sel[...]
+            if k > 0:
+                one(k, h).wait_send()
+            else:
+                pl.when(first_tile + h != t)(lambda h=h: one(0, h).wait_send())
+
+    def landed(p, n, at, count):
+        part = land.at[p, :, pl.ds(at, count)]
+        pltpu.make_async_copy(part, part, recv_two.at[p, n]).wait()
+
+    for p in range(low):
+        landed(p, 0, 3, rows)
+        pl.when(has_down)(functools.partial(landed, p, 1, 3 + rows, 3))
+        pl.when(has_up)(functools.partial(landed, p, 2, 0, 3))
+
+    out_ref[...] = land[lax.rem(sources[0], low)]
+
+    for k in range(low):
+        if k > 0:
+            across(k).wait_send()
+        pl.when(has_up)(lambda k=k: up(k).wait_send())
+        pl.when(has_down)(lambda k=k: down(k).wait_send())
 
 
 def route(n_req, n_tile, piece_dest, latents):
     slots, channels, cols = latents.shape
     rows = slots // LFRAMES
+    far = n_req // 2 if n_req < 8 else 4
+    low = n_req // far
     return pl.pallas_call(
         functools.partial(route_kernel, n_req, n_tile),
         out_shape=jax.ShapeDtypeStruct((LFRAMES, rows + 6, channels, cols), BF16),
@@ -169,13 +178,14 @@
         out_specs=pl.BlockSpec(memory_space=pltpu.VMEM),
         scratch_shapes=[
             pltpu.SMEM(piece_dest.shape, jnp.int32),
-            pltpu.VMEM((n_req, LFRAMES, rows, channels, cols), BF16),
-            pltpu.VMEM((LFRAMES, rows + 6, channels, cols), BF16),
+            pltpu.VMEM((far, LFRAMES, rows, channels, cols), BF16),
+            pltpu.VMEM((low, LFRAMES, rows, channels, cols), BF16),
+            pltpu.VMEM((low, LFRAMES, rows + 6, channels, cols), BF16),
             pltpu.SemaphoreType.DMA,
-            pltpu.SemaphoreType.DMA((n_req, 2)),
-            pltpu.SemaphoreType.DMA((n_req, LFRAMES)),
-            pltpu.SemaphoreType.DMA((2,)),
-            pltpu.SemaphoreType.DMA((2,)),
+            pltpu.SemaphoreType.DMA((far, 2)),
+            pltpu.SemaphoreType.DMA((far, LFRAMES)),
+            pltpu.SemaphoreType.DMA((low, 3)),
+            pltpu.SemaphoreType.DMA((low, 3)),
         ],
         compiler_params=pltpu.CompilerParams(
             collective_id=0, has_side_effects=True, vmem_limit_bytes=VMEM_BYTES
@@ -203,8 +213,8 @@
     vector_hbm, (w_res_hbm, w_time_hbm, w_up_hbm) = hbm[4:9], hbm[9:]
     frames_ref, heights_ref, widths_ref, *refs = refs
     vectors, refs = refs[:5], refs[5:]
-    taps, w_in, wr, wt, wu_raw, wu, x_in, first, spread, timed, inter, perm, *refs = refs
-    c_in, c_gain, c_res, c_time, c_up, sem_s, sem_v, sem_i, sem_r, sem_t, sem_u = refs
+    taps, w_in, wr, wt, wu_raw, wu, x_in, first, spread, timed, inter, result, perm, *refs = refs
+    c_in, c_gain, c_res, c_time, c_up, sem_s, sem_v, sem_i, sem_r, sem_t, sem_u, sem_o = refs
     g = lax.axis_index("req")
     t = lax.axis_index("tile")
     channels, cols = grid_ref.shape[2], grid_ref.shape[3]
@@ -249,11 +259,8 @@
     for copy in copies_s + copies_v + copies_i + copies_r + copies_t + [copy_u]:
         copy.start()
 
-    for copy in copies_s + copies_v + copies_i:
+    for copy in copies_s:
         copy.wait()
-    w_in[...] = jnp.transpose(taps[...])
-    for kept, vector in zip((c_in, c_gain, c_res, c_time, c_up), vectors):
-        kept[...] = column(vector)
     src = lax.broadcasted_iota(jnp.int32, (2 * cols, 2 * cols), 0)
     dst = lax.broadcasted_iota(jnp.int32, (2 * cols, 2 * cols), 1)
     perm[...] = jnp.where(
@@ -285,10 +292,16 @@
                         at = base + (d * 3 + e) * channels
                         x_in[at : at + channels, (q - d) * cols : (q - d + 1) * cols] = y
 
+    for copy in copies_v + copies_i:
+        copy.wait()
+    w_in[...] = jnp.transpose(taps[...])
+    for kept, vector in zip((c_in, c_gain, c_res, c_time, c_up), vectors):
+        kept[...] = column(vector)
+
     span = mrows // 2
 
     def stage_first(p, carry):
-        at = pl.multiple_of(p * span * cols, span * cols)
+        at = p * span * cols
         here = pl.ds(at, span * cols)
         for f in range(LFRAMES):
             if f == 0:
@@ -301,7 +314,7 @@
             v = half.astype(F32)
             mean = jnp.sum(v * v, axis=0, keepdims=True) * (1.0 / mid)
             v = v * lax.rsqrt(mean + 1e-06) * wide(c_gain, span)
-            v = v / (1.0 + jnp.exp(-v))
+            v = 0.5 * v * (1.0 + jnp.tanh(0.5 * v))
             v = jnp.where(masks(f, rows * t - 2 + span * p, span), v, 0.0)
             parts = [v[:, i * cols : (i + 1) * cols] for i in range(span)]
             for e in range(3):
@@ -311,7 +324,8 @@
                 ).astype(BF16)
         return carry
 
-    lax.fori_loop(0, 2, stage_first, 0)
+    for p in range(2):
+        stage_first(p, 0)
 
     for copy in copies_r + copies_t:
         copy.wait()
@@ -374,12 +388,15 @@
                         :, w * cols : (w + 1) * cols
                     ]
         for w in range(2):
-            out_ref[0, :, f, :, w * cols : (w + 1) * cols] = (
+            result[f, :, :, w * cols : (w + 1) * cols] = (
                 inter[w].reshape(outc, 2 * rows, cols).astype(BF16)
             )
+        pltpu.make_async_copy(result.at[f], out_ref.at[0, :, f], sem_o.at[f]).start()
         return carry
 
-    lax.fori_loop(0, 2 * LFRAMES, stage_up, 0)
+    lax.fori_loop(0, 2 * LFRAMES, stage_up, 0, unroll=2)
+    for f in range(2 * LFRAMES):
+        pltpu.make_async_copy(result.at[f], out_ref.at[0, :, f], sem_o.at[f]).wait()
 
 
 def decode(grid, frames, heights, widths, w_in, vectors, w_res, w_time, w_up):
@@ -391,7 +408,7 @@
         decode_kernel,
         out_shape=jax.ShapeDtypeStruct((1, outc, 2 * LFRAMES, 2 * rows, 2 * cols), BF16),
         in_specs=[vmem] + [pl.BlockSpec(memory_space=pltpu.HBM)] * 12,
-        out_specs=vmem,
+        out_specs=pl.BlockSpec(memory_space=pltpu.HBM),
         scratch_shapes=[pltpu.SMEM(v.shape, jnp.int32) for v in (frames, heights, widths)]
         + [pltpu.VMEM(v.shape, F32) for v in vectors]
         + [
@@ -406,6 +423,7 @@
             pltpu.VMEM((6 * mid, (rows + 4) * cols), BF16),
             pltpu.VMEM((2 * LFRAMES, mid, (rows + 2) * cols), BF16),
             pltpu.VMEM((2, outc * 2 * rows, cols), F32),
+            pltpu.VMEM((2 * LFRAMES, outc, 2 * rows, 2 * cols), BF16),
             pltpu.VMEM((2 * cols, 2 * cols), BF16),
             pltpu.VMEM((mid, 128), F32),
             pltpu.VMEM((mid, 128), F32),
@@ -418,6 +436,7 @@
             pltpu.SemaphoreType.DMA((3, 6)),
             pltpu.SemaphoreType.DMA((2,)),
             pltpu.SemaphoreType.DMA,
+            pltpu.SemaphoreType.DMA((2 * LFRAMES,)),
         ],
         compiler_params=pltpu.CompilerParams(vmem_limit_bytes=VMEM_BYTES),
         name="decode",

time: 41.1 us -> 37.8 us (0.920)
  Pallas kernels: 40.7 us -> 37.3 us
    pallas_call x1, Pallas kernels: 25.4 us -> 23.3 us  [decode(): pl.pallas_call(decode_kernel, out_shape=jax.ShapeDtypeStruct((1, outc, 2...]
    pallas_call x1, Pallas kernels: 15.3 us -> 14 us  [route(): pl.pallas_call(functools.partial(route_kernel, n_req, n_tile), out_shape=...]
where the time goes in v3:
time: 37.8 us; the launch traced here: 37.5 us
  Pallas kernels  37.3 us (99%)
    pallas_call x1, Pallas kernels, decode(): pl.pallas_call(decode_kernel, out_shape=jax.ShapeDtypeStruct((1, outc, 2...  23.3 us
    pallas_call x1, Pallas kernels, route(): pl.pallas_call(functools.partial(route_kernel, n_req, n_tile), out_shape=...  14 us

profile of v3, /device:TPU:1, one launch (start us, length us, event | category | flops | bytes accessed | tf_op | source)
XLA Modules:
  0.0 37.5 jit_solution(16342114762018156316)
XLA Ops:
  0.0 14.0 %route.1.grid_ref = bf16[2,10,16,128]{3,2,1,0:T(8,128)(2,1)} custom-call(s32[256]{0:T(256)} %dest_hbm.1, bf16[8,16,128]{2,1,0:T(8,128)(2,1)} %lat_ref.1), custom_call_target="tpu_custom_call" | custom-call | tf_op jit(solution)/shard_map/route/pallas_call | solution.py:174
  14.0 23.3 %decode.1 = bf16[1,192,4,8,256]{4,3,2,1,0:T(8,128)(2,1)} custom-call(bf16[2,10,16,128]{3,2,1,0:T(8,128)(2,1)} %route.1.grid_ref, s32[8]{0:T(128)} %refs_0_.1, s32[8]{0:T(128)} %refs_1_.1, s32[8]{0:T(128)} %refs_2_.1, bf16[432,384]{1,0:T(8,128)(2,1)} %bitcast.3, f32[384]{0:T(512)} %refs_4_.1, f32[384]{0:T(512)} %refs_5_.1, f32[384]{0:T(512)} %refs_6_.1, ...), custom_call_target="tpu_custom_call" | custom-call | tf_op jit(solution)/shard_map/decode/pallas_call | solution.py:407

commit v4 on v3

--- a/solution.py
+++ b/solution.py
@@ -261,18 +261,18 @@
 
     for copy in copies_s:
         copy.wait()
-    src = lax.broadcasted_iota(jnp.int32, (2 * cols, 2 * cols), 0)
-    dst = lax.broadcasted_iota(jnp.int32, (2 * cols, 2 * cols), 1)
-    perm[...] = jnp.where(
-        (src % cols == dst // 2) & (src // cols == dst % 2), 1.0, 0.0
-    ).astype(BF16)
-
     n_frames, n_rows, n_cols = frames_ref[g], heights_ref[g], widths_ref[g]
     lane = lax.broadcasted_iota(jnp.int32, (1, cols), 1)
 
     def mask(f, r):
         live = (f < n_frames) & (r >= 0) & (r < n_rows)
         return lane < jnp.where(live, n_cols, 0)
+
+    src = lax.broadcasted_iota(jnp.int32, (2 * cols, 2 * cols), 0)
+    dst = lax.broadcasted_iota(jnp.int32, (2 * cols, 2 * cols), 1)
+    pick = (src % cols == dst // 2) & (src // cols == dst % 2) & (dst // 2 < n_cols)
+    perm[0] = jnp.where(pick, 1.0, 0.0).astype(BF16)
+    perm[1] = jnp.zeros((2 * cols, 2 * cols), BF16)
 
     def masks(f, r, n):
         return jnp.concatenate([mask(f, r + i) for i in range(n)], axis=1)
@@ -300,72 +300,48 @@
 
     span = mrows // 2
 
-    def stage_first(p, carry):
+    def stage_first(f, p):
         at = p * span * cols
         here = pl.ds(at, span * cols)
-        for f in range(LFRAMES):
-            if f == 0:
-                x = x_in[one : 2 * one, here]
-            else:
-                x = x_in[:, here]
-            acc = jnp.dot(w_in[:, 0 : x.shape[0]], x, preferred_element_type=F32)
-            half = (acc + wide(c_in, span)).astype(BF16)
-            first[f, :, here] = half
-            v = half.astype(F32)
-            mean = jnp.sum(v * v, axis=0, keepdims=True) * (1.0 / mid)
-            v = v * lax.rsqrt(mean + 1e-06) * wide(c_gain, span)
-            v = 0.5 * v * (1.0 + jnp.tanh(0.5 * v))
-            v = jnp.where(masks(f, rows * t - 2 + span * p, span), v, 0.0)
-            parts = [v[:, i * cols : (i + 1) * cols] for i in range(span)]
-            for e in range(3):
-                moved = parts if e == 1 else [shift(part, 1 - e) for part in parts]
-                spread[(f * 3 + e) * mid : (f * 3 + e + 1) * mid, here] = jnp.concatenate(
-                    moved, axis=1
-                ).astype(BF16)
-        return carry
-
-    for p in range(2):
-        stage_first(p, 0)
-
-    for copy in copies_r + copies_t:
-        copy.wait()
+        x = x_in[one : 2 * one, here] if f == 0 else x_in[:, here]
+        acc = jnp.dot(w_in[:, 0 : x.shape[0]], x, preferred_element_type=F32)
+        half = (acc + wide(c_in, span)).astype(BF16)
+        first[f, :, here] = half
+        v = half.astype(F32)
+        mean = jnp.sum(v * v, axis=0, keepdims=True) * (1.0 / mid)
+        v = v * lax.rsqrt(mean + 1e-06) * wide(c_gain, span)
+        v = 0.5 * v * (1.0 + jnp.tanh(0.5 * v))
+        v = jnp.where(masks(f, rows * t - 2 + span * p, span), v, 0.0)
+        parts = [v[:, i * cols : (i + 1) * cols] for i in range(span)]
+        for e in range(3):
+            moved = parts if e == 1 else [shift(part, 1 - e) for part in parts]
+            spread[(f * 3 + e) * mid : (f * 3 + e + 1) * mid, here] = jnp.concatenate(
+                moved, axis=1
+            ).astype(BF16)
 
     brows = rows + 2
-    taller = [
-        jnp.concatenate(
+
+    def taller(f):
+        return jnp.concatenate(
             [
                 spread[f * 3 * mid : (f + 1) * 3 * mid, d * cols : (d + brows) * cols]
                 for d in range(3)
             ],
             axis=0,
         )
-        for f in range(LFRAMES)
-    ]
-    old = jnp.dot(wr[...], taller[0], preferred_element_type=F32)
-    new = jnp.dot(wr[0:mid], taller[1], preferred_element_type=F32)
-    blocks = []
-    for f, acc in enumerate((old[0:mid], old[mid:] + new)):
+
+    def stage_block(f, acc):
         kept = first[f, :, cols : (brows + 1) * cols].astype(F32)
-        blocks.append((acc + wide(c_res, brows) + kept).astype(BF16))
-    for f in range(LFRAMES):
-        if f == 0:
-            twice = jnp.dot(wt[:, mid:], blocks[0], preferred_element_type=F32)
-        else:
-            both = jnp.concatenate(blocks, axis=0)
-            twice = jnp.dot(wt[...], both, preferred_element_type=F32)
+        return (acc + wide(c_res, brows) + kept).astype(BF16)
+
+    def stage_time(f, x):
+        twice = jnp.dot(wt[:, 2 * mid - x.shape[0] :], x, preferred_element_type=F32)
         live = masks(f, rows * t - 1, brows)
         twice = jnp.where(live, twice + wide(c_time, brows), 0.0).astype(BF16)
         for k in range(2):
             timed[2 * f + k] = twice[k * mid : (k + 1) * mid]
 
-    copy_u.wait()
-    w0, w1, w2 = [wu_raw[d].reshape(3 * outc, mid) for d in range(3)]
-    wu[0, :, 0:mid] = w0
-    wu[0, :, mid:] = (w1.astype(F32) + w2.astype(F32)).astype(BF16)
-    wu[1, :, 0:mid] = (w0.astype(F32) + w1.astype(F32)).astype(BF16)
-    wu[1, :, mid:] = w2
-
-    def stage_up(f, carry):
+    def stage_up(f):
         x = [timed[f, :, i * cols : (i + rows) * cols] for i in range(3)]
         for k in range(2):
             z = jnp.dot(
@@ -377,24 +353,44 @@
                 z0, z1, z2 = [
                     z[e * outc : (e + 1) * outc, r * cols : (r + 1) * cols] for e in range(3)
                 ]
-                live = mask(f // 2, rows * t + r)
+                live = (f // 2 < n_frames) & (rows * t + r < n_rows)
                 base = z1 + c_up[...]
-                even = jnp.where(live, shift(z0, 1) + z2 + base, 0.0)
-                odd = jnp.where(live, z0 + shift(z2, -1) + base, 0.0)
-                pair = jnp.concatenate([even, odd], axis=1).astype(BF16)
-                row = jnp.dot(pair, perm[...], preferred_element_type=F32)
+                even = (shift(z0, 1) + z2 + base).astype(BF16)
+                odd = (z0 + shift(z2, -1) + base).astype(BF16)
+                pair = jnp.concatenate([even, odd], axis=1)
+                row = jnp.dot(pair, perm[jnp.where(live, 0, 1)], preferred_element_type=F32)
                 for w in range(2):
-                    inter[w, pl.ds(2 * r + k, outc, stride=2 * rows), :] = row[
+                    inter[f % 2, w, pl.ds(2 * r + k, outc, stride=2 * rows), :] = row[
                         :, w * cols : (w + 1) * cols
                     ]
         for w in range(2):
             result[f, :, :, w * cols : (w + 1) * cols] = (
-                inter[w].reshape(outc, 2 * rows, cols).astype(BF16)
+                inter[f % 2, w].reshape(outc, 2 * rows, cols).astype(BF16)
             )
         pltpu.make_async_copy(result.at[f], out_ref.at[0, :, f], sem_o.at[f]).start()
-        return carry
-
-    lax.fori_loop(0, 2 * LFRAMES, stage_up, 0, unroll=2)
+
+
+    for p in range(2):
+        stage_first(0, p)
+    for copy in copies_r + copies_t + [copy_u]:
+        copy.wait()
+    old = jnp.dot(wr[...], taller(0), preferred_element_type=F32)
+    for p in range(2):
+        stage_first(1, p)
+    w0, w1, w2 = [wu_raw[d].reshape(3 * outc, mid) for d in range(3)]
+    wu[0, :, 0:mid] = w0
+    wu[0, :, mid:] = (w1.astype(F32) + w2.astype(F32)).astype(BF16)
+    wu[1, :, 0:mid] = (w0.astype(F32) + w1.astype(F32)).astype(BF16)
+    wu[1, :, mid:] = w2
+
+    block0 = stage_block(0, old[0:mid])
+    stage_time(0, block0)
+    new = jnp.dot(wr[0:mid], taller(1), preferred_element_type=F32)
+    stage_up(0)
+    block1 = stage_block(1, old[mid:] + new)
+    stage_time(1, jnp.concatenate([block0, block1], axis=0))
+    for f in range(1, 2 * LFRAMES):
+        stage_up(f)
     for f in range(2 * LFRAMES):
         pltpu.make_async_copy(result.at[f], out_ref.at[0, :, f], sem_o.at[f]).wait()
 
@@ -422,9 +418,9 @@
             pltpu.VMEM((LFRAMES, mid, (rows + 4) * cols), BF16),
             pltpu.VMEM((6 * mid, (rows + 4) * cols), BF16),
             pltpu.VMEM((2 * LFRAMES, mid, (rows + 2) * cols), BF16),
-            pltpu.VMEM((2, outc * 2 * rows, cols), F32),
+            pltpu.VMEM((2, 2, outc * 2 * rows, cols), F32),
             pltpu.VMEM((2 * LFRAMES, outc, 2 * rows, 2 * cols), BF16),
-            pltpu.VMEM((2 * cols, 2 * cols), BF16),
+            pltpu.VMEM((2, 2 * cols, 2 * cols), BF16),
             pltpu.VMEM((mid, 128), F32),
             pltpu.VMEM((mid, 128), F32),
             pltpu.VMEM((mid, 128), F32),

time: 37.8 us -> 37 us (0.979)
  Pallas kernels: 37.3 us -> 36.6 us
    pallas_call x1, Pallas kernels: 23.3 us -> 22.6 us  [decode(): pl.pallas_call(decode_kernel, out_shape=jax.ShapeDtypeStruct((1, outc, 2...]
where the time goes in v4:
time: 37 us; the launch traced here: 36.6 us
  Pallas kernels  36.6 us (99%)
    pallas_call x1, Pallas kernels, decode(): pl.pallas_call(decode_kernel, out_shape=jax.ShapeDtypeStruct((1, outc, 2...  22.6 us
    pallas_call x1, Pallas kernels, route(): pl.pallas_call(functools.partial(route_kernel, n_req, n_tile), out_shape=...  14 us

profile of v4, /device:TPU:1, one launch (start us, length us, event | category | flops | bytes accessed | tf_op | source)
XLA Modules:
  0.0 36.6 jit_solution(15486974746481235384)
XLA Ops:
  0.0 14.0 %route.1.grid_ref = bf16[2,10,16,128]{3,2,1,0:T(8,128)(2,1)} custom-call(s32[256]{0:T(256)} %dest_hbm.1, bf16[8,16,128]{2,1,0:T(8,128)(2,1)} %lat_ref.1), custom_call_target="tpu_custom_call" | custom-call | tf_op jit(solution)/shard_map/route/pallas_call | solution.py:174
  14.0 22.6 %decode.1 = bf16[1,192,4,8,256]{4,3,2,1,0:T(8,128)(2,1)} custom-call(bf16[2,10,16,128]{3,2,1,0:T(8,128)(2,1)} %route.1.grid_ref, s32[8]{0:T(128)} %refs_0_.1, s32[8]{0:T(128)} %refs_1_.1, s32[8]{0:T(128)} %refs_2_.1, bf16[432,384]{1,0:T(8,128)(2,1)} %bitcast.3, f32[384]{0:T(512)} %refs_4_.1, f32[384]{0:T(512)} %refs_5_.1, f32[384]{0:T(512)} %refs_6_.1, ...), custom_call_target="tpu_custom_call" | custom-call | tf_op jit(solution)/shard_map/decode/pallas_call | solution.py:403

commit v5 on v4

--- a/solution.py
+++ b/solution.py
@@ -213,7 +213,7 @@
     vector_hbm, (w_res_hbm, w_time_hbm, w_up_hbm) = hbm[4:9], hbm[9:]
     frames_ref, heights_ref, widths_ref, *refs = refs
     vectors, refs = refs[:5], refs[5:]
-    taps, w_in, wr, wt, wu_raw, wu, x_in, first, spread, timed, inter, result, perm, *refs = refs
+    taps, w_in, wr, wt, wu_raw, wu, x_in, first, spread, timed, result, perm, *refs = refs
     c_in, c_gain, c_res, c_time, c_up, sem_s, sem_v, sem_i, sem_r, sem_t, sem_u, sem_o = refs
     g = lax.axis_index("req")
     t = lax.axis_index("tile")
@@ -271,8 +271,7 @@
     src = lax.broadcasted_iota(jnp.int32, (2 * cols, 2 * cols), 0)
     dst = lax.broadcasted_iota(jnp.int32, (2 * cols, 2 * cols), 1)
     pick = (src % cols == dst // 2) & (src // cols == dst % 2) & (dst // 2 < n_cols)
-    perm[0] = jnp.where(pick, 1.0, 0.0).astype(BF16)
-    perm[1] = jnp.zeros((2 * cols, 2 * cols), BF16)
+    perm[...] = jnp.where(pick, 1.0, 0.0).astype(BF16)
 
     def masks(f, r, n):
         return jnp.concatenate([mask(f, r + i) for i in range(n)], axis=1)
@@ -343,6 +342,7 @@
 
     def stage_up(f):
         x = [timed[f, :, i * cols : (i + rows) * cols] for i in range(3)]
+        pairs = [None] * (2 * rows)
         for k in range(2):
             z = jnp.dot(
                 wu[k],
@@ -358,15 +358,10 @@
                 even = (shift(z0, 1) + z2 + base).astype(BF16)
                 odd = (z0 + shift(z2, -1) + base).astype(BF16)
                 pair = jnp.concatenate([even, odd], axis=1)
-                row = jnp.dot(pair, perm[jnp.where(live, 0, 1)], preferred_element_type=F32)
-                for w in range(2):
-                    inter[f % 2, w, pl.ds(2 * r + k, outc, stride=2 * rows), :] = row[
-                        :, w * cols : (w + 1) * cols
-                    ]
-        for w in range(2):
-            result[f, :, :, w * cols : (w + 1) * cols] = (
-                inter[f % 2, w].reshape(outc, 2 * rows, cols).astype(BF16)
-            )
+                pairs[2 * r + k] = jnp.where(live, pair, jnp.zeros_like(pair))
+        woven = jnp.dot(jnp.concatenate(pairs, axis=0), perm[...], preferred_element_type=F32)
+        woven = woven.reshape(2 * rows, outc, 2 * cols)
+        result[f] = jnp.transpose(woven, (1, 0, 2)).astype(BF16)
         pltpu.make_async_copy(result.at[f], out_ref.at[0, :, f], sem_o.at[f]).start()
 
 
@@ -418,9 +413,8 @@
             pltpu.VMEM((LFRAMES, mid, (rows + 4) * cols), BF16),
             pltpu.VMEM((6 * mid, (rows + 4) * cols), BF16),
             pltpu.VMEM((2 * LFRAMES, mid, (rows + 2) * cols), BF16),
-            pltpu.VMEM((2, 2, outc * 2 * rows, cols), F32),
             pltpu.VMEM((2 * LFRAMES, outc, 2 * rows, 2 * cols), BF16),
-            pltpu.VMEM((2, 2 * cols, 2 * cols), BF16),
+            pltpu.VMEM((2 * cols, 2 * cols), BF16),
             pltpu.VMEM((mid, 128), F32),
             pltpu.VMEM((mid, 128), F32),
             pltpu.VMEM((mid, 128), F32),

time: 37 us -> 36 us (0.973)
  Pallas kernels: 36.6 us -> 35.6 us
    pallas_call x1, Pallas kernels: 22.6 us -> 21.6 us  [decode(): pl.pallas_call(decode_kernel, out_shape=jax.ShapeDtypeStruct((1, outc, 2...]
where the time goes in v5:
time: 36 us; the launch traced here: 35.6 us
  Pallas kernels  35.6 us (99%)
    pallas_call x1, Pallas kernels, decode(): pl.pallas_call(decode_kernel, out_shape=jax.ShapeDtypeStruct((1, outc, 2...  21.6 us
    pallas_call x1, Pallas kernels, route(): pl.pallas_call(functools.partial(route_kernel, n_req, n_tile), out_shape=...  14 us

profile of v5, /device:TPU:1, one launch (start us, length us, event | category | flops | bytes accessed | tf_op | source)
XLA Modules:
  0.0 35.6 jit_solution(17822924392629989676)
XLA Ops:
  0.0 14.0 %route.1.grid_ref = bf16[2,10,16,128]{3,2,1,0:T(8,128)(2,1)} custom-call(s32[256]{0:T(256)} %dest_hbm.1, bf16[8,16,128]{2,1,0:T(8,128)(2,1)} %lat_ref.1), custom_call_target="tpu_custom_call" | custom-call | tf_op jit(solution)/shard_map/route/pallas_call | solution.py:174
  14.0 21.6 %decode.1 = bf16[1,192,4,8,256]{4,3,2,1,0:T(8,128)(2,1)} custom-call(bf16[2,10,16,128]{3,2,1,0:T(8,128)(2,1)} %route.1.grid_ref, s32[8]{0:T(128)} %refs_0_.1, s32[8]{0:T(128)} %refs_1_.1, s32[8]{0:T(128)} %refs_2_.1, bf16[432,384]{1,0:T(8,128)(2,1)} %bitcast.3, f32[384]{0:T(512)} %refs_4_.1, f32[384]{0:T(512)} %refs_5_.1, f32[384]{0:T(512)} %refs_6_.1, ...), custom_call_target="tpu_custom_call" | custom-call | tf_op jit(solution)/shard_map/decode/pallas_call | solution.py:398

commit v6 on v5

--- a/solution.py
+++ b/solution.py
@@ -367,11 +367,13 @@
 
     for p in range(2):
         stage_first(0, p)
-    for copy in copies_r + copies_t + [copy_u]:
+    for copy in copies_r:
         copy.wait()
     old = jnp.dot(wr[...], taller(0), preferred_element_type=F32)
     for p in range(2):
         stage_first(1, p)
+    for copy in copies_t + [copy_u]:
+        copy.wait()
     w0, w1, w2 = [wu_raw[d].reshape(3 * outc, mid) for d in range(3)]
     wu[0, :, 0:mid] = w0
     wu[0, :, mid:] = (w1.astype(F32) + w2.astype(F32)).astype(BF16)

time: 36 us -> 37.4 us (1.039)
  Pallas kernels: 35.6 us -> 36.9 us
    pallas_call x1, Pallas kernels: 21.6 us -> 22.9 us  [decode(): pl.pallas_call(decode_kernel, out_shape=jax.ShapeDtypeStruct((1, outc, 2...]
where the time goes in v6:
time: 37.4 us; the launch traced here: 37.1 us
  Pallas kernels  36.9 us (99%)
    pallas_call x1, Pallas kernels, decode(): pl.pallas_call(decode_kernel, out_shape=jax.ShapeDtypeStruct((1, outc, 2...  22.9 us
    pallas_call x1, Pallas kernels, route(): pl.pallas_call(functools.partial(route_kernel, n_req, n_tile), out_shape=...  14 us

profile of v6, /device:TPU:1, one launch (start us, length us, event | category | flops | bytes accessed | tf_op | source)
XLA Modules:
  0.0 37.1 jit_solution(10433697075462283440)
XLA Ops:
  0.0 14.0 %route.1.grid_ref = bf16[2,10,16,128]{3,2,1,0:T(8,128)(2,1)} custom-call(s32[256]{0:T(256)} %dest_hbm.1, bf16[8,16,128]{2,1,0:T(8,128)(2,1)} %lat_ref.1), custom_call_target="tpu_custom_call" | custom-call | tf_op jit(solution)/shard_map/route/pallas_call | solution.py:174
  14.0 22.9 %decode.1 = bf16[1,192,4,8,256]{4,3,2,1,0:T(8,128)(2,1)} custom-call(bf16[2,10,16,128]{3,2,1,0:T(8,128)(2,1)} %route.1.grid_ref, s32[8]{0:T(128)} %refs_0_.1, s32[8]{0:T(128)} %refs_1_.1, s32[8]{0:T(128)} %refs_2_.1, bf16[432,384]{1,0:T(8,128)(2,1)} %bitcast.3, f32[384]{0:T(512)} %refs_4_.1, f32[384]{0:T(512)} %refs_5_.1, f32[384]{0:T(512)} %refs_6_.1, ...), custom_call_target="tpu_custom_call" | custom-call | tf_op jit(solution)/shard_map/decode/pallas_call | solution.py:400
